TPU v7x, 256 devices: a whole 4x4x8 slice. The times are simulated.
256 devices in a mesh: store: 16 (over y, x), batch: 8 (over z), space: 2 (over core).
Axes of the slice: x: 4, y: 4, z: 8, core: 2. Of those that a mesh axis runs over, the one named last changes fastest.
Arguments:
- features: bfloat16 [512, 256, 1024], P(('store', 'batch'), 'space'), may hold values from -24 to 24
- store_maps: bfloat16 [64, 256, 1024], P('store', 'space'), may hold values from -17 to 17
- neighbour_owner: int32 [512, 2], P(('store', 'batch')), may hold values from 0 to 15, all different within a row; in each aligned block of 4 rows (0 to 3, 4 to 7, ...) at most 2 rows name the same one
- neighbour_slot: int32 [512, 2], P(('store', 'batch')), may hold values from 0 to 3
- query_weight: bfloat16 [1024, 1024], P('store', 'space'), may hold values from -0.1875 to 0.1875
- key_weight: bfloat16 [1024, 1024], P('store', 'space'), may hold values from -0.1875 to 0.1875
- value_weight: bfloat16 [1024, 1024], P('store', 'space'), may hold values from -0.1875 to 0.1875
- grad_context: bfloat16 [512, 256, 1024], P(('store', 'batch'), 'space'), may hold values from -6 to 6
Outputs:
- grad_features: bfloat16 [512, 256, 1024], P(('store', 'batch'), 'space')
- grad_query: float32 [1024, 1024], P('store', 'space')
- grad_key: float32 [1024, 1024], P('store', 'space')
- grad_value: float32 [1024, 1024], P('store', 'space')
Inputs may be any that keep to these rules, and one draw needn't show every extreme that they name: `neighbour_owner`: within the 4 prompts of one store and batch index, each owner is listed by at most 2 prompts; a prompt's two neighbours have different owners.
All inputs are finite; a program needn't handle non-finite values.
Results may differ from a plain program's by a relative error of at most 0.017.
The roundings to bfloat16 on the way count: a program that leaves them out, or rounds other values in their place, can miss the bound.
Values may be sent and summed in bfloat16 or wider, within the bound.
No kernel may reach another device: no remote copies, remote signals or barrier semaphores. Data moves between devices by JAX's collectives and lax.ppermute only.
A program may use at most 128 MiB of HBM per device.

v0:
```python
import jax
import jax.numpy as jnp
from jax import lax
from jax.sharding import PartitionSpec as P

HD = 64


def per_device(
    features,
    store_maps,
    neighbour_owner,
    neighbour_slot,
    query_weight,
    key_weight,
    value_weight,
    grad_context,
):
    prompts, quarter, channels = features.shape
    entries = store_maps.shape[0]
    owners = lax.axis_size("store")
    most_listed = max(2, (2 * prompts + owners - 1) // owners)
    slot_count = owners * most_listed
    score_scale = HD ** (-0.5)
    full_query, full_key, full_value = (
        lax.all_gather(query_weight, "store", axis=0, tiled=True),
        lax.all_gather(key_weight, "store", axis=0, tiled=True),
        lax.all_gather(value_weight, "store", axis=0, tiled=True),
    )
    prompt_rows = lax.all_gather(features, "space", axis=1, tiled=True)
    tokens = prompt_rows.shape[1]
    wanted = neighbour_owner.reshape(-1)
    picked = neighbour_slot.reshape(-1)
    listed = wanted.shape[0]
    position = jnp.arange(listed, dtype=jnp.int32)
    earlier = (wanted[:, None] == wanted[None, :]) & (position[None, :] < position[:, None])
    slot_rank = jnp.sum(earlier.astype(jnp.int32), axis=1)
    target = wanted * most_listed + slot_rank
    placed = target[:, None] == jnp.arange(slot_count, dtype=jnp.int32)[None, :]
    requests = jnp.sum(jnp.where(placed, picked[:, None] + 1, 0), axis=0).reshape(
        owners, most_listed
    )
    incoming = lax.all_to_all(requests, "store", split_axis=0, concat_axis=0, tiled=True)
    lookup = (
        incoming.reshape(-1)[:, None] == jnp.arange(1, entries + 1, dtype=jnp.int32)[None, :]
    ).astype(jnp.bfloat16)
    served = jnp.dot(
        lookup, store_maps.reshape(entries, -1), preferred_element_type=jnp.float32
    ).astype(jnp.bfloat16)
    served = served.reshape(owners, most_listed, quarter, channels)
    returned = lax.all_to_all(served, "store", split_axis=0, concat_axis=0, tiled=True)
    chosen = jnp.dot(
        placed.astype(jnp.bfloat16),
        returned.reshape(slot_count, -1),
        preferred_element_type=jnp.float32,
    ).astype(jnp.bfloat16)
    chosen = chosen.reshape(prompts, 2, quarter, channels)
    neighbours = lax.all_gather(chosen, "space", axis=2, tiled=True)
    key_rows = neighbours.reshape(prompts * 2 * tokens, channels)
    query = jnp.dot(
        prompt_rows.reshape(-1, channels), full_query, preferred_element_type=jnp.float32
    ).astype(jnp.bfloat16)
    keys = jnp.dot(key_rows, full_key, preferred_element_type=jnp.float32).astype(jnp.bfloat16)
    values = jnp.dot(key_rows, full_value, preferred_element_type=jnp.float32).astype(jnp.bfloat16)
    local_width = query.shape[1]
    head_count = local_width // HD
    query_heads = query.reshape(prompts, tokens, head_count, HD)
    key_heads = keys.reshape(prompts, 2 * tokens, head_count, HD)
    value_heads = values.reshape(prompts, 2 * tokens, head_count, HD)
    scores = (
        jnp.einsum("pthd,pshd->phts", query_heads, key_heads, preferred_element_type=jnp.float32)
        * score_scale
    )
    attention = jax.nn.softmax(scores, axis=-1)
    weights = attention.astype(jnp.bfloat16)
    upstream = lax.all_to_all(
        grad_context, "space", split_axis=2, concat_axis=1, tiled=True
    ).reshape(prompts, tokens, head_count, HD)
    dweights = jnp.einsum(
        "pthd,pshd->phts", upstream, value_heads, preferred_element_type=jnp.float32
    )
    grad_values = jnp.einsum(
        "phts,pthd->pshd", weights, upstream, preferred_element_type=jnp.float32
    ).astype(jnp.bfloat16)
    dscores = (
        attention * (dweights - jnp.sum(attention * dweights, axis=-1, keepdims=True))
    ).astype(jnp.bfloat16)
    grad_query_rows = (
        jnp.einsum("phts,pshd->pthd", dscores, key_heads, preferred_element_type=jnp.float32)
        * score_scale
    ).astype(jnp.bfloat16)
    grad_keys = (
        jnp.einsum("phts,pthd->pshd", dscores, query_heads, preferred_element_type=jnp.float32)
        * score_scale
    ).astype(jnp.bfloat16)
    contract = (((0,), (0,)), ((), ()))
    flat_query_grad = grad_query_rows.reshape(prompts * tokens, local_width)
    grad_q_local = lax.dot_general(
        prompt_rows.reshape(-1, channels),
        flat_query_grad,
        contract,
        preferred_element_type=jnp.float32,
    )
    grad_k_local = lax.dot_general(
        key_rows, grad_keys.reshape(-1, local_width), contract, preferred_element_type=jnp.float32
    )
    grad_v_local = lax.dot_general(
        key_rows, grad_values.reshape(-1, local_width), contract, preferred_element_type=jnp.float32
    )
    token_major = jnp.transpose(grad_query_rows.reshape(prompts, tokens, local_width), (1, 0, 2))
    summed_rows = lax.psum_scatter(
        jnp.einsum(
            "tpi,ci->tpc", token_major, full_query, preferred_element_type=jnp.float32
        ).astype(jnp.bfloat16),
        "space",
        scatter_dimension=0,
        tiled=True,
    ).astype(jnp.float32)
    grad_features = jnp.transpose(summed_rows, (1, 0, 2)).astype(jnp.bfloat16)
    row_share = channels // owners
    totals = lax.psum((grad_q_local, grad_k_local, grad_v_local), ("store", "batch"))
    begin = lax.axis_index("store") * row_share
    grad_query = lax.dynamic_slice_in_dim(totals[0], begin, row_share, 0)
    grad_key = lax.dynamic_slice_in_dim(totals[1], begin, row_share, 0)
    grad_value = lax.dynamic_slice_in_dim(totals[2], begin, row_share, 0)
    return (grad_features, grad_query, grad_key, grad_value)


def solution(mesh):
    in_specs = (
        P(("store", "batch"), "space", None),
        P("store", "space", None),
        P(("store", "batch"), None),
        P(("store", "batch"), None),
        P("store", "space"),
        P("store", "space"),
        P("store", "space"),
        P(("store", "batch"), "space", None),
    )
    out_specs = (
        P(("store", "batch"), "space", None),
        P("store", "space"),
        P("store", "space"),
        P("store", "space"),
    )
    return jax.shard_map(
        per_device, mesh=mesh, in_specs=in_specs, out_specs=out_specs, check_vma=False
    )
```

profile of v0, /device:TPU:4, one launch (start us, length us, event | category | flops | bytes accessed | tf_op | source)
XLA Modules:
  0.0 651.8 jit_solution(15105880314172400703)
XLA Ops:
  7.2 0.8 copy.59
  8.2 0.7 broadcast_add_fusion
  9.2 0.7 all_to_all.20
  9.9 7.4 %all-to-all-start = ((s32[16,1,2]{2,1,0:T(1,128)}), s32[16,1,2]{2,1,0:T(1,128)S(1)}, u32[]{:S(2)}, u32[]{:S(2)}) async-start(s32[16,1,2]{2,1,0:T(1,128)} %bitcast), calls=%async_computation | async-start | bytes 16384 | tf_op jit(solution)/shard_map/all_to_all | solution.py:43
  17.3 2.0 copy.85
  19.4 3.2 all-to-all-done
  23.8 5.6 convolution_convert_fusion
  29.4 11.4 %copy.86 = bf16[4,8,128,1024]{3,2,1,0:T(8,128)(2,1)} copy(bf16[4,8,128,1024]{3,1,2,0:T(8,128)(2,1)} %bitcast.86) | data formatting | bytes 16777216
  40.8 6.8 %all-to-all-start.1 = ((bf16[16,2,128,1024]{3,2,1,0:T(8,128)(2,1)}), bf16[16,2,128,1024]{3,2,1,0:T(8,128)(2,1)}, u32[]{:S(2)}, u32[]{:S(2)}) async-start(bf16[16,2,128,1024]{3,2,1,0:T(8,128)(2,1)} %bitcast.85), calls=%async_computation.1 | async-start | bytes 16777216 | tf_op jit(solution)/shard_map/all_to_all | solution.py:51
  47.6 0.7 all-gather.12.cloned.1.call-update
  48.4 0.7 all-gather.10.cloned.1.call-update
  50.0 120.1 %all-to-all-done.1 = bf16[16,2,128,1024]{3,2,1,0:T(8,128)(2,1)} async-done(((bf16[16,2,128,1024]{3,2,1,0:T(8,128)(2,1)}), bf16[16,2,128,1024]{3,2,1,0:T(8,128)(2,1)}, u32[]{:S(2)}, u32[]{:S(2)}) %all-to-all-start.1) | async-done | bytes 8388640 | tf_op jit(solution)/shard_map/all_to_all | solution.py:51
  170.1 11.4 %copy.87 = bf16[4,8,128,1024]{3,1,2,0:T(8,128)(2,1)} copy(bf16[4,8,128,1024]{3,2,1,0:T(8,128)(2,1)} %bitcast.21) | data formatting | bytes 16777216
  181.6 4.7 convolution_convert_fusion.1
  186.3 2.5 copy.88
  189.4 0.8 copy.67
  190.2 5.0 all_to_all.29
  195.1 1.1 copy.97
  196.2 1.5 reshape.97
  197.7 3.1 convolution_convert_fusion.5
  200.8 1.1 reshape.105
  201.9 1.2 copy.64
  203.1 37.2 %all-gather.8.cloned.1.call-done = bf16[1024,512]{1,0:T(8,128)(2,1)} async-done(((bf16[64,512]{1,0:T(8,128)(2,1)}), bf16[1024,512]{1,0:T(8,128)(2,1)}) %all-gather.8.cloned.1.call-update) | async-done | bytes 1048592 | tf_op jit(solution)/shard_map/all_gather | solution.py:27
  240.3 20.6 %all-gather.6.cloned.1.call-done = bf16[4,2,256,1024]{3,2,1,0:T(8,128)(2,1)} async-done(((bf16[4,2,128,1024]{3,2,1,0:T(8,128)(2,1)}), bf16[4,2,256,1024]{3,2,1,0:T(8,128)(2,1)}) %all-gather.6.cloned.1.call-update) | async-done | bytes 4194320 | tf_op jit(solution)/shard_map/all_gather | solution.py:58
  260.9 4.8 convolution_convert_fusion.3
  265.7 3.6 reshape.104
  269.4 4.5 copy.71
  273.8 37.8 %all-gather.14.cloned.1.call-done = bf16[1024,512]{1,0:T(8,128)(2,1)} async-done(((bf16[64,512]{1,0:T(8,128)(2,1)}), bf16[1024,512]{1,0:T(8,128)(2,1)}) %all-gather.14.cloned.1.call-update) | async-done | bytes 1048592 | tf_op jit(solution)/shard_map/all_gather | solution.py:28
  311.6 6.2 convolution_convert_fusion.2
  317.8 6.2 reshape.103
  323.9 8.4 %fusion.25 = (f32[4,8,256]{2,1,0:T(8,128)S(1)}, f32[4,8,256,512]{3,2,1,0:T(8,128)}) fusion(bf16[4,256,8,64]{1,3,2,0:T(8,128)(2,1)S(1)} %copy.64, bf16[4,512,8,64]{1,3,2,0:T(8,128)(2,1)S(1)} %copy.71), kind=kOutput, calls=%fused_computation.46 | convolution fusion | flops 549454336 | bytes 19955712 | tf_op jit(solution)/shard_map/sub | solution.py:74
  332.3 13.4 %fusion.1 = (f32[4,8,256]{2,1,0:T(8,128)S(1)}, f32[4,8,512,256]{2,3,1,0:T(8,128)}) fusion(f32[4,8,256,512]{3,2,1,0:T(8,128)} %get-tuple-element.24, f32[4,8,256]{2,1,0:T(8,128)S(1)} %get-tuple-element.23, bf16[4,256,8,64]{1,3,2,0:T(8,128)(2,1)} %reshape.97, bf16[4,512,8,64]{3,2,1,0:T(8,128)(2,1)} %reshape.103), kind=kOutput, calls=%fused_computation.5 | convolution fusion | flops 549445632 | bytes 36765696 | tf_op jit(solution)/shard_map/pthd,pshd->phts/dot_general | solution.py:79
  345.7 11.5 %fusion.3 = bf16[4,8,256,512]{3,2,1,0:T(8,128)(2,1)S(1)} fusion(f32[4,8,512,256]{2,3,1,0:T(8,128)} %get-tuple-element.26, f32[4,8,256]{2,1,0:T(8,128)S(1)} %get-tuple-element.25, f32[4,8,256,512]{3,2,1,0:T(8,128)} %get-tuple-element.24, f32[4,8,256]{2,1,0:T(8,128)S(1)} %get-tuple-element.23), kind=kLoop, calls=%fused_computation.7 | loop fusion | flops 16777216 | bytes 42008576 | tf_op jit(solution)/shard_map/convert_element_type | solution.py:87
  357.3 1.5 fusion.14
  358.8 2.7 multiply_convert_fusion.1
  361.5 6.7 %convert_bitcast_fusion = bf16[4,512,8,64]{1,3,2,0:T(8,128)(2,1)S(1)} fusion(bf16[4,256,8,64]{1,3,2,0:T(8,128)(2,1)S(1)} %copy-done.1, f32[4,8,256,512]{3,2,1,0:T(8,128)} %get-tuple-element.24, f32[4,8,256]{2,1,0:T(8,128)S(1)} %get-tuple-element.23), kind=kOutput, calls=%fused_computation.20 | convolution fusion | flops 546308096 | bytes 19955712 | tf_op jit(solution)/shard_map/phts,pthd->pshd/dot_general | solution.py:82
  368.2 1.6 copy.75
  370.5 3.7 fusion.26
  374.2 0.8 copy.73
  375.8 2.6 convolution_bitcast_fusion
  378.5 1.6 copy.76
  380.7 3.7 fusion.27
  385.7 2.6 convolution_convert_fusion.4
  388.3 240.5 %all-reduce.3.cloned.1.call-done = (f32[1024,512]{0,1:T(8,128)}, f32[1024,512]{1,0:T(8,128)}, f32[1024,512]{1,0:T(8,128)}) async-done(((f32[1024,512]{0,1:T(8,128)}, f32[1024,512]{1,0:T(8,128)}, f32[1024,512]{1,0:T(8,128)}), (f32[1024,512]{0,1:T(8,128)}, f32[1024,512]{1,0:T(8,128)}, f32[1024,512]{1,0:T(8,128)})) %all-reduce.3.cloned.1.call-update) | async-done | bytes 6291472 | tf_op jit(solution)/shard_map/psum | solution.py:121
  628.8 1.1 constant_dynamic-slice_fusion.2
  629.9 0.8 copy.77
  630.7 1.7 constant_dynamic-slice_fusion
  632.3 12.4 %reduce-scatter.2.cloned.1.call-done = bf16[128,4,1024]{2,0,1:T(8,128)(2,1)} async-done(((bf16[256,4,1024]{2,0,1:T(8,128)(2,1)}), bf16[128,4,1024]{2,0,1:T(8,128)(2,1)}) %reduce-scatter.2.cloned.1.call-update) | async-done | bytes 1048592 | tf_op jit(solution)/shard_map/reduce_scatter | solution.py:111
  (38 shorter events, 6.7 us)
Async XLA Ops:
  9.9 12.7 %all-to-all-start = ((s32[16,1,2]{2,1,0:T(1,128)}), s32[16,1,2]{2,1,0:T(1,128)S(1)}, u32[]{:S(2)}, u32[]{:S(2)}) async-start(s32[16,1,2]{2,1,0:T(1,128)} %bitcast), calls=%async_computation | async-start | bytes 16384 | tf_op jit(solution)/shard_map/all_to_all | solution.py:43
  40.8 129.3 %all-to-all-start.1 = ((bf16[16,2,128,1024]{3,2,1,0:T(8,128)(2,1)}), bf16[16,2,128,1024]{3,2,1,0:T(8,128)(2,1)}, u32[]{:S(2)}, u32[]{:S(2)}) async-start(bf16[16,2,128,1024]{3,2,1,0:T(8,128)(2,1)} %bitcast.85), calls=%async_computation.1 | async-start | bytes 16777216 | tf_op jit(solution)/shard_map/all_to_all | solution.py:51
  47.6 150.1 %all-gather.12.cloned.1.call-start = ((), (), s32[]{:S(2)}) async-start(), calls=%async_computation.7 | async-start | bytes 1114112 | tf_op jit(solution)/shard_map/all_gather | solution.py:26
  48.3 149.4 %all-gather.10.cloned.1.call-start = ((), (), s32[]{:S(2)}) async-start(), calls=%async_computation.6 | async-start | bytes 3145728 | tf_op jit(solution)/shard_map/all_gather | solution.py:30
  49.1 191.2 %all-gather.8.cloned.1.call-start = ((), (), s32[]{:S(2)}) async-start(), calls=%async_computation.5 | async-start | bytes 1114112 | tf_op jit(solution)/shard_map/all_gather | solution.py:27
  49.8 211.1 %all-gather.6.cloned.1.call-start = ((), (), s32[]{:S(2)}) async-start(), calls=%async_computation.4 | async-start | bytes 6291456 | tf_op jit(solution)/shard_map/all_gather | solution.py:58
  186.3 3.1 copy-start
  188.8 122.9 %all-gather.14.cloned.1.call-start = ((), (), s32[]{:S(2)}) async-start(), calls=%async_computation.8 | async-start | bytes 1114112 | tf_op jit(solution)/shard_map/all_gather | solution.py:28
  189.4 439.4 %all-reduce.3.cloned.1.call-start = ((), (), s32[]{:S(2)}) async-start(), calls=%async_computation.10 | async-start | bytes 12582912 | tf_op jit(solution)/shard_map/psum | solution.py:121
  358.8 2.7 copy-start.1
  368.2 2.3 copy-start.2
  374.2 1.6 copy-start.3
  384.5 1.2 copy-start.4
  384.5 260.3 %reduce-scatter.2.cloned.1.call-start = ((), (), s32[]{:S(2)}) async-start(), calls=%async_computation.9 | async-start | bytes 3145728 | tf_op jit(solution)/shard_map/reduce_scatter | solution.py:111
Sparse Core Ops, SparseCore 0:
  50.9 116.6 all-gather.11
  169.4 19.9 all-gather.9
  191.8 48.4 all-gather.7
  242.0 18.8 all-gather.5
  263.2 48.4 all-gather.13
  384.6 244.1 all-reduce.2
  631.9 12.8 reduce-scatter.1
where the time goes:
time: 660 us; the launch traced here: 652 us
  waiting for transfers between devices  474 us (72%)
  matrix products  69.8 us (11%)
  local copies, waits for them, and re-layouts  60.2 us (9%)
  starting transfers between devices  14.7 us (2%)
  between operations  14.5 us (2%)
  other arithmetic  13.2 us (2%)
    psum x1, waiting for transfers between devices, per_device(): lax.psum((grad_q_local, grad_k_local, grad_v_local), ('store', 'batch'))  240 us
    all_to_all x1, waiting for transfers between devices, per_device(): lax.all_to_all(served, 'store', split_axis=0, concat_axis=0, tiled=True)  120 us
    all_gather x1, waiting for transfers between devices, per_device(): lax.all_gather(value_weight, 'store', axis=0, tiled=True)  37.8 us
    all_gather x1, waiting for transfers between devices, per_device(): lax.all_gather(key_weight, 'store', axis=0, tiled=True)  37.2 us
    unnamed x20, local copies, waits for them, and re-layouts  32.2 us
    all_gather x1, waiting for transfers between devices, per_device(): neighbours = lax.all_gather(chosen, 'space', axis=2, tiled=True)  20.6 us
    dot_general x1, matrix products, per_device(): jnp.einsum('pthd,pshd->phts', upstream, value_heads, preferred_element_ty...  13.4 us
  transfers between devices with their start and end apart: 9, of which 7 were waited for; matrix products, arithmetic and copies ran while one was open for 8% of the time, Pallas kernels for 0%

commit v1 on v0

v1 whole, which is shorter than its diff:
```python
import functools

import jax
import jax.numpy as jnp
from jax import lax
from jax.experimental import pallas as pl
from jax.experimental.pallas import tpu as pltpu
from jax.sharding import PartitionSpec as P

HD = 64
F32 = jnp.float32
BF16 = jnp.bfloat16
NT = (((1,), (1,)), ((), ()))
TN = (((0,), (0,)), ((), ()))


def pick_kernel(where_ref, table_ref, *outs):
    layers, per = outs[0].shape[:2]
    for number, out in enumerate(outs):
        for layer in range(layers):
            for item in range(per):
                place = where_ref[(number * layers + layer) * per + item]
                out[layer, item] = table_ref[place]


def pick(table, where, chunks, layers, per):
    rows, channels = table.shape[1:]
    vmem = pl.BlockSpec(memory_space=pltpu.VMEM)
    return pl.pallas_call(
        pick_kernel,
        out_shape=[jax.ShapeDtypeStruct((layers, per, rows, channels), table.dtype)] * chunks,
        in_specs=[pl.BlockSpec(memory_space=pltpu.SMEM), vmem],
        out_specs=[vmem] * chunks,
        compiler_params=pltpu.CompilerParams(vmem_limit_bytes=16 * 2**20),
        name="pick",
    )(where, table)


def attention_kernel(
    xo, xt, uo, ut, no, nt, wq, wk, wv, gq, gk, gv, q_s, k_s, v_s, u_s
):
    half = xo.shape[1]
    tokens = 2 * half
    layers, _, rows, channels = no.shape
    part = layers * rows
    own, other = no[...].reshape(part, channels), nt[...].reshape(part, channels)
    q_s[:half] = jnp.dot(xo[0], wq[...], preferred_element_type=F32).astype(BF16)
    q_s[half:] = jnp.dot(xt[0], wq[...], preferred_element_type=F32).astype(BF16)
    k_s[:part] = jnp.dot(own, wk[...], preferred_element_type=F32).astype(BF16)
    k_s[part:] = jnp.dot(other, wk[...], preferred_element_type=F32).astype(BF16)
    v_s[:part] = jnp.dot(own, wv[...], preferred_element_type=F32).astype(BF16)
    v_s[part:] = jnp.dot(other, wv[...], preferred_element_type=F32).astype(BF16)
    u_s[:half] = uo[0]
    u_s[half:] = ut[0]
    width = q_s.shape[1]
    scale = HD ** (-0.5)
    lane = lax.broadcasted_iota(jnp.int32, (1, 2 * HD), 1)
    first = lane < HD
    for pair in range(width // (2 * HD)):
        cols = pl.ds(pair * 2 * HD, 2 * HD)
        kp, vp = k_s[:, cols], v_s[:, cols]
        grad_k = grad_v = None
        grad_q = []
        for side in range(2):
            keep = jnp.where(first if side == 0 else jnp.logical_not(first), 1.0, 0.0)
            qm = q_s[:, cols] * (keep * scale).astype(BF16)
            um = u_s[:, cols] * keep.astype(BF16)
            s = lax.dot_general(kp, qm, NT, preferred_element_type=F32)
            e = jnp.exp(s - jnp.max(s, axis=0, keepdims=True))
            att = e * (1.0 / jnp.sum(e, axis=0, keepdims=True))
            dw = lax.dot_general(vp, um, NT, preferred_element_type=F32)
            gv_part = jnp.dot(att.astype(BF16), um, preferred_element_type=F32)
            row = jnp.sum(att * dw, axis=0, keepdims=True)
            ds = (att * (dw - row)).astype(BF16)
            gk_part = jnp.dot(ds, qm, preferred_element_type=F32)
            grad_q.append(lax.dot_general(ds, kp, TN, preferred_element_type=F32))
            grad_v = gv_part if grad_v is None else grad_v + gv_part
            grad_k = gk_part if grad_k is None else grad_k + gk_part
        gq[0, :, cols] = (jnp.where(first, grad_q[0], grad_q[1]) * scale).astype(BF16)
        gk[0, :, cols] = grad_k.astype(BF16)
        gv[0, :, cols] = grad_v.astype(BF16)


def attention(xo, xt, uo, ut, no, nt, weights, first_prompt):
    layers, prompts, rows, channels = no.shape
    part = layers * rows
    half = xo.shape[1]
    local = weights.shape[1] // 3
    step = min(local, 4 * HD)
    steps = local // step
    token_spec = pl.BlockSpec((1, half, channels), lambda p, c: (p + first_prompt, 0, 0))
    up_spec = pl.BlockSpec((1, half, step), lambda p, c: (p + first_prompt, 0, c))
    map_spec = pl.BlockSpec((layers, 1, rows, channels), lambda p, c: (0, p, 0, 0))
    w_specs = [
        pl.BlockSpec((channels, step), lambda p, c, i=i: (0, c + i * steps)) for i in range(3)
    ]
    flops = prompts * 2 * (2 * half * channels * local + 4 * part * channels * local) + (
        prompts * 2 * local * 5 * 2 * half * 2 * part
    )
    return pl.pallas_call(
        attention_kernel,
        grid=(prompts, steps),
        out_shape=[
            jax.ShapeDtypeStruct((prompts, 2 * half, local), BF16),
            jax.ShapeDtypeStruct((prompts, 2 * part, local), BF16),
            jax.ShapeDtypeStruct((prompts, 2 * part, local), BF16),
        ],
        in_specs=[token_spec, token_spec, up_spec, up_spec, map_spec, map_spec] + w_specs,
        out_specs=[
            pl.BlockSpec((1, 2 * half, step), lambda p, c: (p, 0, c)),
            pl.BlockSpec((1, 2 * part, step), lambda p, c: (p, 0, c)),
            pl.BlockSpec((1, 2 * part, step), lambda p, c: (p, 0, c)),
        ],
        scratch_shapes=[
            pltpu.VMEM((2 * half, step), BF16),
            pltpu.VMEM((2 * part, step), BF16),
            pltpu.VMEM((2 * part, step), BF16),
            pltpu.VMEM((2 * half, step), BF16),
        ],
        compiler_params=pltpu.CompilerParams(vmem_limit_bytes=40 * 2**20),
        cost_estimate=pl.CostEstimate(
            flops=2 * flops, bytes_accessed=12 * 2**20, transcendentals=prompts * 2**20
        ),
        name="attention",
    )(xo, xt, uo, ut, no, nt, weights, weights, weights)


def hold(array, after):
    anywhere = pl.BlockSpec(memory_space=pl.ANY)
    return pl.pallas_call(
        lambda array_ref, after_ref, out_ref: None,
        out_shape=jax.ShapeDtypeStruct(array.shape, array.dtype),
        in_specs=[anywhere, anywhere],
        out_specs=anywhere,
        input_output_aliases={0: 0},
        name="hold",
    )(array, after)


def weights_kernel(first_prompt, keep, *refs):
    xo, xt, no, nt, gq, gk, gv = refs[:7]
    before, out = (None, refs[7]) if keep else (refs[7], refs[8])
    prompts = gq.shape[0]
    layers, _, rows, width = no.shape
    local = gq.shape[2]
    tokens, maps = [], []
    for p in range(prompts):
        tokens += [xo[first_prompt + p], xt[first_prompt + p]]
        maps += [no[:, p].reshape(layers * rows, width), nt[:, p].reshape(layers * rows, width)]
    tokens, maps = jnp.concatenate(tokens, axis=0), jnp.concatenate(maps, axis=0)
    for i, (left, grad) in enumerate(((tokens, gq), (maps, gk), (maps, gv))):
        cols = pl.ds(i * local, local)
        total = lax.dot_general(
            left, grad[...].reshape(-1, local), TN, preferred_element_type=F32
        )
        if before is not None:
            total = total + before[:, cols]
        out[:, cols] = total.astype(out.dtype)


def weight_grads(xo, xt, no, nt, gq, gk, gv, before, first_prompt):
    prompts, half, channels = xo.shape
    layers, per_chunk, rows, _ = no.shape
    local = gq.shape[2]
    width = 256
    keep = before is None
    token_spec = pl.BlockSpec((prompts, half, width), lambda c: (0, 0, c))
    map_spec = pl.BlockSpec((layers, per_chunk, rows, width), lambda c: (0, 0, 0, c))
    grad_specs = [pl.BlockSpec(g.shape, lambda c: (0, 0, 0)) for g in (gq, gk, gv)]
    out_spec = pl.BlockSpec((width, 3 * local), lambda c: (c, 0))
    extra = [] if keep else [before]
    return pl.pallas_call(
        functools.partial(weights_kernel, first_prompt, keep),
        grid=(channels // width,),
        out_shape=jax.ShapeDtypeStruct((channels, 3 * local), F32 if keep else BF16),
        in_specs=[token_spec, token_spec, map_spec, map_spec]
        + grad_specs
        + [out_spec] * len(extra),
        out_specs=out_spec,
        compiler_params=pltpu.CompilerParams(vmem_limit_bytes=40 * 2**20),
        cost_estimate=pl.CostEstimate(
            flops=2 * channels * local * per_chunk * (2 * half + 4 * layers * rows),
            bytes_accessed=12 * 2**20,
            transcendentals=0,
        ),
        name="weight_grads",
    )(xo, xt, no, nt, gq, gk, gv, *extra)


def per_device(
    features,
    store_maps,
    neighbour_owner,
    neighbour_slot,
    query_weight,
    key_weight,
    value_weight,
    grad_context,
):
    prompts, half, channels = features.shape
    entries = store_maps.shape[0]
    owners = lax.axis_size("store")
    layers = lax.axis_size("batch")
    local = query_weight.shape[1]
    layer, core = lax.axis_index("batch"), lax.axis_index("space")
    swap = [(0, 1), (1, 0)]

    share = half // layers
    mine = lax.dynamic_slice_in_dim(store_maps, layer * share, share, axis=1)
    table = lax.all_to_all(
        jnp.broadcast_to(mine[None], (owners,) + mine.shape),
        "store",
        split_axis=0,
        concat_axis=0,
        tiled=True,
    ).reshape(owners * entries, share, channels)

    listed = (neighbour_owner * entries + neighbour_slot).reshape(1, -1)
    reach = 1
    while reach < layers:
        moved = lax.ppermute(
            listed, "batch", [(z, (z + reach) % layers) for z in range(layers)]
        )
        listed = jnp.concatenate([listed, moved], axis=0)
        reach *= 2
    place = jnp.roll(listed[::-1], layer + 1, axis=0)
    chunks = 2
    per_chunk = prompts // chunks
    per = 2 * per_chunk
    order = place.reshape(layers, chunks, per).transpose(1, 0, 2).reshape(-1)
    picked = pick(table, order, chunks, layers, per)

    packed = jnp.concatenate([query_weight, key_weight, value_weight], axis=1)
    weights = lax.all_gather(packed, "store", axis=0, tiled=True)
    full_query = weights[:, :local]

    x_other = lax.ppermute(features, "space", swap)
    u_own = lax.dynamic_slice_in_dim(grad_context, core * local, local, axis=2)
    u_send = lax.dynamic_slice_in_dim(grad_context, (1 - core) * local, local, axis=2)
    u_other = lax.ppermute(u_send, "space", swap)

    sums = gq = None
    features_out = []
    for chunk in range(chunks):
        n_own = lax.all_to_all(
            picked[chunk], "batch", split_axis=0, concat_axis=0, tiled=True
        ).reshape(layers, per_chunk, 2 * share, channels)
        if gq is not None:
            n_own = hold(n_own, gq)
        n_other = lax.ppermute(n_own, "space", swap)
        begin = chunk * per_chunk
        gq, gk, gv = attention(
            features, x_other, u_own, u_other, n_own, n_other, weights, begin
        )
        part = half * 2
        partial_rows = jnp.dot(
            gq.reshape(per_chunk * part, local).reshape(per_chunk, 2, half, local),
            full_query.T,
            preferred_element_type=F32,
        ).astype(BF16)
        received = lax.ppermute(partial_rows[:, 1], "space", swap)
        features_out.append(
            (partial_rows[:, 0].astype(F32) + received.astype(F32)).astype(BF16)
        )

        sums = weight_grads(features, x_other, n_own, n_other, gq, gk, gv, sums, begin)
    grad_features = jnp.concatenate(features_out, axis=0)

    row_share = channels // owners
    sent = sums.reshape(owners, row_share, 3 * local)
    came = lax.all_to_all(sent, "store", split_axis=0, concat_axis=0, tiled=True)
    layer_sum = jnp.sum(came.astype(F32), axis=0)
    pieces = layer_sum.reshape(layers, row_share // layers, 3 * local)
    crossed = lax.all_to_all(pieces, "batch", split_axis=0, concat_axis=0, tiled=True)
    summed = jnp.sum(crossed, axis=0, keepdims=True)
    totals = lax.all_to_all(
        jnp.broadcast_to(summed, pieces.shape), "batch", split_axis=0, concat_axis=0, tiled=True
    ).reshape(row_share, 3 * local)
    return (
        grad_features,
        totals[:, :local],
        totals[:, local : 2 * local],
        totals[:, 2 * local :],
    )


def solution(mesh):
    in_specs = (
        P(("store", "batch"), "space", None),
        P("store", "space", None),
        P(("store", "batch"), None),
        P(("store", "batch"), None),
        P("store", "space"),
        P("store", "space"),
        P("store", "space"),
        P(("store", "batch"), "space", None),
    )
    out_specs = (
        P(("store", "batch"), "space", None),
        P("store", "space"),
        P("store", "space"),
        P("store", "space"),
    )
    return jax.shard_map(
        per_device, mesh=mesh, in_specs=in_specs, out_specs=out_specs, check_vma=False
    )
```

time: 660 us -> 264 us (0.40)
  waiting for transfers between devices: 474 us -> 87.5 us
  matrix products: 69.8 us -> 3.92 us
  Pallas kernels: 0 us -> 44.3 us
  local copies, waits for them, and re-layouts: 60.2 us -> 27.4 us
  blocking collectives: 4.96 us -> 37.4 us
  starting transfers between devices: 14.7 us -> 36.1 us
    psum x1 -> x0, waiting for transfers between devices: 240 us -> none  [per_device(): lax.psum((grad_q_local, grad_k_local, grad_v_local), ('store', 'batch'))]
    all_gather x5 -> x1, waiting for transfers between devices: 95.6 us -> 0.01 us  [per_device(): weights = lax.all_gather(packed, 'store', axis=0, tiled=True)]
    dot_general x13 -> x2, matrix products: 61.4 us -> 3.92 us  [per_device(): jnp.dot(gq.reshape(per_chunk * part, local).reshape(per_chunk, 2, half, l...]
    all_to_all x2 -> x5, waiting for transfers between devices: 123 us -> 71.2 us  [the longest x1 41 us: per_device(): lax.all_to_all(sent, 'store', split_axis=0, concat_axis=0, tiled=True)]
    pallas_call x0 -> x6, Pallas kernels: none -> 44.3 us  [the longest x2 32.7 us: attention(): pl.pallas_call(attention_kernel, grid=(prompts, steps), out_shape=[jax.Sh...]
    all_to_all x1, blocking collectives: 4.96 us -> 37.4 us  [per_device(): lax.all_to_all(picked[chunk], 'batch', split_axis=0, concat_axis=0, tiled...]
    reshape x8 -> x2, local copies, waits for them, and re-layouts: 18.6 us -> 0.17 us  [the longest x1 0.09 us: per_device(): order = place.reshape(layers, chunks, per).transpose(1, 0, 2).reshape(-1)]
    ppermute x0 -> x9, waiting for transfers between devices: none -> 16.3 us  [the longest x3 14 us: per_device(): lax.ppermute(listed, 'batch', [(z, (z + reach) % layers) for z in range(l...]
  transfers between devices with their start and end apart: 9 -> 15, of which waited for: 7 -> 8; matrix products, arithmetic and copies ran while one was open for 8% -> 7% of each run, Pallas kernels for 0% -> 9%
where the time goes in v1:
time: 264 us; the launch traced here: 259 us
  waiting for transfers between devices  87.5 us (33%)
  Pallas kernels  44.3 us (17%)
  blocking collectives  37.4 us (14%)
  starting transfers between devices  36.1 us (14%)
  local copies, waits for them, and re-layouts  27.4 us (10%)
  between operations  14.4 us (5%)
  other arithmetic  8.39 us (3%)
  matrix products  3.92 us (1%)
    all_to_all x1, waiting for transfers between devices, per_device(): lax.all_to_all(sent, 'store', split_axis=0, concat_axis=0, tiled=True)  41 us
    all_to_all x1, blocking collectives, per_device(): lax.all_to_all(picked[chunk], 'batch', split_axis=0, concat_axis=0, tiled...  37.4 us
    pallas_call x2, Pallas kernels, attention(): pl.pallas_call(attention_kernel, grid=(prompts, steps), out_shape=[jax.Sh...  32.7 us
    unnamed x56, local copies, waits for them, and re-layouts  20 us
    ppermute x3, waiting for transfers between devices, per_device(): lax.ppermute(listed, 'batch', [(z, (z + reach) % layers) for z in range(l...  14 us
    all_to_all x1, waiting for transfers between devices, per_device(): lax.all_to_all(pieces, 'batch', split_axis=0, concat_axis=0, tiled=True)  11.3 us
    pallas_call x2, Pallas kernels, weight_grads(): pl.pallas_call(functools.partial(weights_kernel, first_prompt, keep), gri...  11 us
    all_to_all x1, waiting for transfers between devices, per_device(): lax.all_to_all(jnp.broadcast_to(summed, pieces.shape), 'batch', split_axi...  9.74 us
  transfers between devices with their start and end apart: 15, of which 8 were waited for; matrix products, arithmetic and copies ran while one was open for 7% of the time, Pallas kernels for 9%

profile of v1, /device:TPU:4, one launch (start us, length us, event | category | flops | bytes accessed | tf_op | source)
XLA Modules:
  0.0 259.5 jit_solution(18371658414615691321)
XLA Ops:
  7.2 1.7 pad_maximum_fusion.1
  9.0 1.6 broadcast_in_dim.4
  10.6 7.4 %all-to-all-start = ((bf16[16,4,16,1024]{3,2,1,0:T(8,128)(2,1)}), bf16[16,4,16,1024]{3,2,1,0:T(8,128)(2,1)S(1)}, u32[]{:S(2)}, u32[]{:S(2)}) async-start(bf16[16,4,16,1024]{3,2,1,0:T(8,128)(2,1)} %broadcast_in_dim.4), calls=%async_computation | async-start | bytes 4194304 | tf_op jit(solution)/shard_map/all_to_all | solution.py:210
  18.2 1.9 collective-permute-start.2
  20.2 5.5 %collective-permute-done.2 = s32[1,8]{1,0:T(1,128)S(1)} collective-permute-done((s32[1,8]{1,0:T(1,128)S(1)}, s32[1,8]{1,0:T(1,128)S(1)}, u32[]{:S(2)}, u32[]{:S(2)}) %collective-permute-start.2) | collective-permute-done | bytes 64 | tf_op jit(solution)/shard_map/ppermute | solution.py:221
  25.7 5.7 %collective-permute-done.3 = s32[2,8]{1,0:T(2,128)S(1)} collective-permute-done((s32[2,8]{1,0:T(2,128)S(1)}, s32[2,8]{1,0:T(2,128)S(1)}, u32[]{:S(2)}, u32[]{:S(2)}) %collective-permute-start.3) | collective-permute-done | bytes 96 | tf_op jit(solution)/shard_map/ppermute | solution.py:221
  31.4 4.7 %collective-permute-start.4 = (s32[4,8]{1,0:T(4,128)S(1)}, s32[4,8]{1,0:T(4,128)S(1)}, u32[]{:S(2)}, u32[]{:S(2)}) collective-permute-start(s32[4,8]{1,0:T(4,128)S(1)} %pad_add_fusion.1), channel_id=1, source_target_pairs={{0,8},{2,10},{4,12},{6,14},{8,0},{10,2},{12,4},{14,6},{1,9},{3,11}... | collective-permute-start | bytes 392 | tf_op jit(solution)/shard_map/ppermute | solution.py:221
  36.0 2.9 %collective-permute-done.4 = s32[4,8]{1,0:T(4,128)S(1)} collective-permute-done((s32[4,8]{1,0:T(4,128)S(1)}, s32[4,8]{1,0:T(4,128)S(1)}, u32[]{:S(2)}, u32[]{:S(2)}) %collective-permute-start.4) | collective-permute-done | bytes 160 | tf_op jit(solution)/shard_map/ppermute | solution.py:221
  39.3 9.2 %all-to-all-done = bf16[16,4,16,1024]{3,2,1,0:T(8,128)(2,1)S(1)} async-done(((bf16[16,4,16,1024]{3,2,1,0:T(8,128)(2,1)}), bf16[16,4,16,1024]{3,2,1,0:T(8,128)(2,1)S(1)}, u32[]{:S(2)}, u32[]{:S(2)}) %all-to-all-start) | async-done | bytes 2097184 | tf_op jit(solution)/shard_map/all_to_all | solution.py:210
  49.2 37.4 %all_to_all.30 = bf16[8,4,16,1024]{3,2,1,0:T(8,128)(2,1)} all-to-all(bf16[8,4,16,1024]{3,2,1,0:T(8,128)(2,1)S(1)} %get-tuple-element.12), channel_id=1, replica_groups=mesh['store'=16,'batch'=8,'space'=2] {'batch'}, dimensions={0} | all-to-all | bytes 2097152 | tf_op jit(solution)/shard_map/all_to_all | solution.py:245
  86.7 3.6 %all-to-all-start.2 = ((bf16[8,4,16,1024]{3,2,1,0:T(8,128)(2,1)}), bf16[8,4,16,1024]{3,2,1,0:T(8,128)(2,1)S(1)}, u32[]{:S(2)}, u32[]{:S(2)}) async-start(bf16[8,4,16,1024]{3,2,1,0:T(8,128)(2,1)} %copy-done.15), calls=%async_computation.2 | async-start | bytes 2097152 | tf_op jit(solution)/shard_map/all_to_all | solution.py:245
  90.8 2.1 constant_dynamic-slice_fusion.1
  93.0 2.2 collective-permute-done.1.ut
  95.2 0.8 copy-done.20
  96.0 1.2 copy-done.6
  97.3 1.0 copy-done.16
  98.3 1.9 copy-done.18
  100.2 1.0 copy-done.21
  101.2 16.4 %attention.2 = (bf16[2,256,512]{2,1,0:T(8,128)(2,1)S(1)}, bf16[2,512,512]{2,1,0:T(8,128)(2,1)S(1)}, bf16[2,512,512]{2,1,0:T(8,128)(2,1)S(1)}) custom-call(bf16[4,128,1024]{2,1,0:T(8,128)(2,1)S(1)} %copy-done.5, bf16[4,128,1024]{2,1,0:T(8,128)(2,1)} %collective-permute-done.xt.refs_1_, bf16[4,128,512]{2,1,0:T(8,128)(2,1)S(1)} %copy-done.16, ...), custom_call_target="tpu_custom_call" | custom-call | flops 8053063680 | bytes 12582912 | tf_op jit(solution)/shard_map/attention/pallas_call | solution.py:100
  117.6 0.8 copy-done.8
  118.4 1.0 copy-done.11
  119.4 1.0 copy-done.13
  120.4 1.0 copy-done.3
  121.5 1.2 copy-done.7
  122.7 1.0 copy-done.9
  123.7 1.2 copy-done.12
  125.0 1.2 copy-done.14
  126.2 5.0 %weight_grads.2.refs_7_ = f32[1024,1536]{1,0:T(8,128)S(1)} custom-call(bf16[4,128,1024]{2,1,0:T(8,128)(2,1)S(1)} %copy-done.5, bf16[4,128,1024]{2,1,0:T(8,128)(2,1)} %collective-permute-done.xt.refs_1_, bf16[8,2,32,1024]{3,2,1,0:T(8,128)(2,1)S(1)} %bitcast.40, bf16[8,2,32,1024]{3,2,1,0:T(8,128)(2,1)} %collective-permute-done.5.nt.refs_3_, ...), custom_call_target="tpu_custom_call" | custom-call | flops 2684354560 | bytes 12582912 | tf_op jit(solution)/shard_map/weight_grads/pallas_call | solution.py:172
  131.2 2.7 %copy-done.1 = f32[1024,1536]{1,0:T(8,128)} copy-done((f32[1024,1536]{1,0:T(8,128)}, f32[1024,1536]{1,0:T(8,128)S(1)}, u32[]{:S(2)}) %copy-start.1) | copy-done | bytes 6291480
  134.0 16.3 %attention.3 = (bf16[2,256,512]{2,1,0:T(8,128)(2,1)S(1)}, bf16[2,512,512]{2,1,0:T(8,128)(2,1)S(1)}, bf16[2,512,512]{2,1,0:T(8,128)(2,1)S(1)}) custom-call(bf16[4,128,1024]{2,1,0:T(8,128)(2,1)S(1)} %copy-done.5, bf16[4,128,1024]{2,1,0:T(8,128)(2,1)} %collective-permute-done.xt.refs_1_, bf16[4,128,512]{2,1,0:T(8,128)(2,1)S(1)} %copy-done.17, ...), custom_call_target="tpu_custom_call" | custom-call | flops 8053063680 | bytes 12582912 | tf_op jit(solution)/shard_map/attention/pallas_call | solution.py:100
  150.3 6.0 %weight_grads.3 = bf16[1024,1536]{1,0:T(8,128)(2,1)S(1)} custom-call(bf16[4,128,1024]{2,1,0:T(8,128)(2,1)S(1)} %copy-done.5, bf16[4,128,1024]{2,1,0:T(8,128)(2,1)} %collective-permute-done.xt.refs_1_, bf16[8,2,32,1024]{3,2,1,0:T(8,128)(2,1)S(1)} %copy-done.4, bf16[8,2,32,1024]{3,2,1,0:T(8,128)(2,1)S(1)} %collective-permute-done.7.nt.refs_3_, ...), custom_call_target="tpu_custom_call" | custom-call | flops 2684354560 | bytes 12582912 | tf_op jit(solution)/shard_map/weight_grads/pallas_call | solution.py:172
  156.2 1.7 copy-done.2
  157.9 7.0 %all-to-all-start.3 = ((bf16[16,64,1536]{2,1,0:T(8,128)(2,1)}), bf16[16,64,1536]{2,1,0:T(8,128)(2,1)}, u32[]{:S(2)}, u32[]{:S(2)}) async-start(bf16[16,64,1536]{2,1,0:T(8,128)(2,1)} %bitcast.35), calls=%async_computation.3 | async-start | bytes 6291456 | tf_op jit(solution)/shard_map/all_to_all | solution.py:271
  164.9 2.0 convolution_convert_fusion.1
  166.9 1.0 copy-done.23
  167.9 0.8 slice_bitcast_fusion.2
  168.8 41.0 %all-to-all-done.3 = bf16[16,64,1536]{2,1,0:T(8,128)(2,1)} async-done(((bf16[16,64,1536]{2,1,0:T(8,128)(2,1)}), bf16[16,64,1536]{2,1,0:T(8,128)(2,1)}, u32[]{:S(2)}, u32[]{:S(2)}) %all-to-all-start.3) | async-done | bytes 3145760 | tf_op jit(solution)/shard_map/all_to_all | solution.py:271
  209.8 3.1 %convert_reduce_fusion = f32[64,1536]{1,0:T(8,128)} fusion(bf16[16,64,1536]{2,1,0:T(8,128)(2,1)} %all-to-all-done.3), kind=kLoop, calls=%fused_computation | loop fusion | flops 3047424 | bytes 3538944 | tf_op jit(solution)/shard_map/reduce_sum | solution.py:272
  212.9 7.0 %all-to-all-start.4 = ((f32[8,8,1536]{2,1,0:T(8,128)}), f32[8,8,1536]{2,1,0:T(8,128)S(1)}, u32[]{:S(2)}, u32[]{:S(2)}) async-start(f32[8,8,1536]{2,1,0:T(8,128)} %bitcast.14), calls=%async_computation.4 | async-start | bytes 786432 | tf_op jit(solution)/shard_map/all_to_all | solution.py:274
  219.9 2.0 convolution_convert_fusion
  221.9 0.9 slice_bitcast_fusion
  223.0 11.3 %all-to-all-done.4 = f32[8,8,1536]{2,1,0:T(8,128)S(1)} async-done(((f32[8,8,1536]{2,1,0:T(8,128)}), f32[8,8,1536]{2,1,0:T(8,128)S(1)}, u32[]{:S(2)}, u32[]{:S(2)}) %all-to-all-start.4) | async-done | bytes 393248 | tf_op jit(solution)/shard_map/all_to_all | solution.py:274
  234.3 0.8 broadcast_in_dim.5
  235.1 3.5 %all-to-all-start.5 = ((f32[8,8,1536]{2,1,0:T(8,128)}), f32[8,8,1536]{2,1,0:T(8,128)S(1)}, u32[]{:S(2)}, u32[]{:S(2)}) async-start(f32[8,8,1536]{2,1,0:T(8,128)} %broadcast_in_dim.5), calls=%async_computation.5 | async-start | bytes 786432 | tf_op jit(solution)/shard_map/all_to_all | solution.py:276
  238.6 1.2 fusion.1
  239.8 1.2 fusion
  241.1 1.1 pad_maximum_fusion
  242.1 9.7 %all-to-all-done.5 = f32[8,8,1536]{2,1,0:T(8,128)S(1)} async-done(((f32[8,8,1536]{2,1,0:T(8,128)}), f32[8,8,1536]{2,1,0:T(8,128)S(1)}, u32[]{:S(2)}, u32[]{:S(2)}) %all-to-all-start.5) | async-done | bytes 393248 | tf_op jit(solution)/shard_map/all_to_all | solution.py:276
  (72 shorter events, 3.4 us)
Async XLA Ops:
  7.2 1.8 copy-start
  7.2 88.8 %all-gather.2.cloned.1.call-start = ((), (), s32[]{:S(2)}) async-start(), calls=%async_computation.6 | async-start | bytes 3342336 | tf_op jit(solution)/shard_map/all_gather | solution.py:234
  9.0 9.1 %copy-start.26 = (s32[4,2]{0,1:T(2,128)S(1)}, s32[4,2]{0,1:T(2,128)}, u32[]{:S(2)}) copy-start(s32[4,2]{0,1:T(2,128)} %param.11) | copy-start | bytes 100
  9.0 9.1 %copy-start.27 = (s32[4,2]{0,1:T(2,128)S(1)}, s32[4,2]{0,1:T(2,128)}, u32[]{:S(2)}) copy-start(s32[4,2]{0,1:T(2,128)} %param.10) | copy-start | bytes 100
  10.6 37.9 %all-to-all-start = ((bf16[16,4,16,1024]{3,2,1,0:T(8,128)(2,1)}), bf16[16,4,16,1024]{3,2,1,0:T(8,128)(2,1)S(1)}, u32[]{:S(2)}, u32[]{:S(2)}) async-start(bf16[16,4,16,1024]{3,2,1,0:T(8,128)(2,1)} %broadcast_in_dim.4), calls=%async_computation | async-start | bytes 4194304 | tf_op jit(solution)/shard_map/all_to_all | solution.py:210
  18.2 7.4 %collective-permute-start.2 = (s32[1,8]{1,0:T(1,128)S(1)}, s32[1,8]{1,0:T(1,128)S(1)}, u32[]{:S(2)}, u32[]{:S(2)}) collective-permute-start(s32[1,8]{1,0:T(1,128)S(1)} %reshape.41), channel_id=1, source_target_pairs={{0,2},{2,4},{4,6},{6,8},{8,10},{10,12},{12,14},{14,0},{1,3},{3,5},... | collective-permute-start | bytes 104 | tf_op jit(solution)/shard_map/ppermute | solution.py:221
  25.6 5.8 %collective-permute-start.3 = (s32[2,8]{1,0:T(2,128)S(1)}, s32[2,8]{1,0:T(2,128)S(1)}, u32[]{:S(2)}, u32[]{:S(2)}) collective-permute-start(s32[2,8]{1,0:T(2,128)S(1)} %pad_add_fusion.2), channel_id=1, source_target_pairs={{0,4},{2,6},{4,8},{6,10},{8,12},{10,14},{12,0},{14,2},{1,5},{3,7},... | collective-permute-start | bytes 200 | tf_op jit(solution)/shard_map/ppermute | solution.py:221
  31.4 7.6 %collective-permute-start.4 = (s32[4,8]{1,0:T(4,128)S(1)}, s32[4,8]{1,0:T(4,128)S(1)}, u32[]{:S(2)}, u32[]{:S(2)}) collective-permute-start(s32[4,8]{1,0:T(4,128)S(1)} %pad_add_fusion.1), channel_id=1, source_target_pairs={{0,8},{2,10},{4,12},{6,14},{8,0},{10,2},{12,4},{14,6},{1,9},{3,11}... | collective-permute-start | bytes 392 | tf_op jit(solution)/shard_map/ppermute | solution.py:221
  49.2 37.5 %copy-start.15 = (bf16[8,4,16,1024]{3,2,1,0:T(8,128)(2,1)}, bf16[8,4,16,1024]{3,2,1,0:T(8,128)(2,1)S(1)}, u32[]{:S(2)}) copy-start(bf16[8,4,16,1024]{3,2,1,0:T(8,128)(2,1)S(1)} %get-tuple-element.14) | copy-start | bytes 3145732
  49.2 41.0 %copy-start.5 = (bf16[4,128,1024]{2,1,0:T(8,128)(2,1)S(1)}, bf16[4,128,1024]{2,1,0:T(8,128)(2,1)}, u32[]{:S(2)}) copy-start(bf16[4,128,1024]{2,1,0:T(8,128)(2,1)} %refs_0_.3) | copy-start | bytes 3145732
  86.7 33.7 %all-to-all-start.2 = ((bf16[8,4,16,1024]{3,2,1,0:T(8,128)(2,1)}), bf16[8,4,16,1024]{3,2,1,0:T(8,128)(2,1)S(1)}, u32[]{:S(2)}, u32[]{:S(2)}) async-start(bf16[8,4,16,1024]{3,2,1,0:T(8,128)(2,1)} %copy-done.15), calls=%async_computation.2 | async-start | bytes 2097152 | tf_op jit(solution)/shard_map/all_to_all | solution.py:245
  90.2 5.8 %collective-permute-start = (bf16[4,128,1024]{2,1,0:T(8,128)(2,1)S(1)}, bf16[4,128,1024]{2,1,0:T(8,128)(2,1)}, u32[]{:S(2)}, u32[]{:S(2)}) collective-permute-start(bf16[4,128,1024]{2,1,0:T(8,128)(2,1)S(1)} %copy-done.5), channel_id=1, source_target_pairs={{0,1},{1,0},{2,3},{3,2},{4,5},{5,4},{6,7},{7,6},{8,9},{9,8},{10,11... | collective-permute-start | bytes 3145736 | tf_op jit(solution)/shard_map/ppermute | solution.py:237
  90.3 5.7 %collective-permute-start.5 = (bf16[8,2,32,1024]{3,2,1,0:T(8,128)(2,1)}, bf16[8,2,32,1024]{3,2,1,0:T(8,128)(2,1)}, u32[]{:S(2)}, u32[]{:S(2)}) collective-permute-start(bf16[8,2,32,1024]{3,2,1,0:T(8,128)(2,1)} %bitcast.38), channel_id=1, source_target_pairs={{0,1},{1,0},{2,3},{3,2},{4,5},{5,4},{6,7},{7,6},{8,9},{9,8},{10,11... | collective-permute-start | bytes 3145736 | tf_op jit(solution)/shard_map/ppermute | solution.py:250
  92.9 2.3 collective-permute-start.1
  95.2 0.8 copy-start.20
  96.0 1.2 copy-start.6
  97.3 1.0 copy-start.16
  98.3 1.9 copy-start.18
  100.2 1.0 copy-start.21
  117.6 0.8 copy-start.8
  118.4 1.0 copy-start.11
  119.4 1.0 copy-start.13
  120.4 1.0 copy-start.3
  121.3 12.6 %collective-permute-start.7 = (bf16[8,2,32,1024]{3,2,1,0:T(8,128)(2,1)}, bf16[8,2,32,1024]{3,2,1,0:T(8,128)(2,1)S(1)}, u32[]{:S(2)}, u32[]{:S(2)}) collective-permute-start(bf16[8,2,32,1024]{3,2,1,0:T(8,128)(2,1)} %hold.1.no.refs_2_), channel_id=1, source_target_pairs={{0,1},{1,0},{2,3},{3,2},{4,5},{5,4},{6,7},{7,6},{8,9},{9,8},{10,11... | collective-permute-start | bytes 3145736 | tf_op jit(solution)/shard_map/ppermute | solution.py:250
  121.5 1.2 copy-start.7
  122.7 1.0 copy-start.9
  123.7 1.2 copy-start.12
  125.0 1.2 copy-start.14
  126.2 7.7 %copy-start.4 = (bf16[8,2,32,1024]{3,2,1,0:T(8,128)(2,1)S(1)}, bf16[8,2,32,1024]{3,2,1,0:T(8,128)(2,1)}, u32[]{:S(2)}) copy-start(bf16[8,2,32,1024]{3,2,1,0:T(8,128)(2,1)} %hold.1.no.refs_2_) | copy-start | bytes 3145732
  126.2 7.7 %copy-start.17 = (bf16[4,128,512]{2,1,0:T(8,128)(2,1)S(1)}, bf16[4,128,512]{2,1,0:T(8,128)(2,1)}, u32[]{:S(2)}) copy-start(bf16[4,128,512]{2,1,0:T(8,128)(2,1)} %get-tuple-element.21.uo) | copy-start | bytes 1572868
  126.2 7.7 %copy-start.19 = (bf16[1024,1536]{1,0:T(8,128)(2,1)S(1)}, bf16[1024,1536]{1,0:T(8,128)(2,1)}, u32[]{:S(2)}) copy-start(bf16[1024,1536]{1,0:T(8,128)(2,1)} %all-gather.2.cloned.1.call-done.wq.wk.wv) | copy-start | bytes 9437188
  126.2 7.8 %copy-start.22 = (bf16[4,128,512]{2,1,0:T(8,128)(2,1)S(1)}, bf16[4,128,512]{2,1,0:T(8,128)(2,1)}, u32[]{:S(2)}) copy-start(bf16[4,128,512]{2,1,0:T(8,128)(2,1)} %copy-done.20) | copy-start | bytes 1572868
  131.2 2.7 %copy-start.1 = (f32[1024,1536]{1,0:T(8,128)}, f32[1024,1536]{1,0:T(8,128)S(1)}, u32[]{:S(2)}) copy-start(f32[1024,1536]{1,0:T(8,128)S(1)} %weight_grads.2.refs_7_) | copy-start | bytes 18874372
  156.2 1.7 copy-start.2
  157.9 7.0 %copy-start.10 = (bf16[2,256,512]{2,1,0:T(8,128)(2,1)S(1)}, bf16[2,256,512]{2,1,0:T(8,128)(2,1)}, u32[]{:S(2)}) copy-start(bf16[2,256,512]{2,1,0:T(8,128)(2,1)} %copy-done.8) | copy-start | bytes 1572868
  157.9 51.9 %all-to-all-start.3 = ((bf16[16,64,1536]{2,1,0:T(8,128)(2,1)}), bf16[16,64,1536]{2,1,0:T(8,128)(2,1)}, u32[]{:S(2)}, u32[]{:S(2)}) async-start(bf16[16,64,1536]{2,1,0:T(8,128)(2,1)} %bitcast.35), calls=%async_computation.3 | async-start | bytes 6291456 | tf_op jit(solution)/shard_map/all_to_all | solution.py:271
  166.9 1.0 copy-start.23
  168.7 69.8 %collective-permute-start.6 = (bf16[2,128,1024]{2,1,0:T(8,128)(2,1)}, bf16[2,128,1024]{2,1,0:T(8,128)(2,1)S(1)}, u32[]{:S(2)}, u32[]{:S(2)}) collective-permute-start(bf16[2,128,1024]{2,1,0:T(8,128)(2,1)} %slice_bitcast_fusion.2), channel_id=1, source_target_pairs={{0,1},{1,0},{2,3},{3,2},{4,5},{5,4},{6,7},{7,6},{8,9},{9,8},{10,11... | collective-permute-start | bytes 1572872 | tf_op jit(solution)/shard_map/ppermute | solution.py:261
  212.9 21.4 %all-to-all-start.4 = ((f32[8,8,1536]{2,1,0:T(8,128)}), f32[8,8,1536]{2,1,0:T(8,128)S(1)}, u32[]{:S(2)}, u32[]{:S(2)}) async-start(f32[8,8,1536]{2,1,0:T(8,128)} %bitcast.14), calls=%async_computation.4 | async-start | bytes 786432 | tf_op jit(solution)/shard_map/all_to_all | solution.py:274
  221.8 1.1 copy-start.24
  223.0 16.8 %collective-permute-start.8 = (bf16[2,128,1024]{2,1,0:T(8,128)(2,1)}, bf16[2,128,1024]{2,1,0:T(8,128)(2,1)}, u32[]{:S(2)}, u32[]{:S(2)}) collective-permute-start(bf16[2,128,1024]{2,1,0:T(8,128)(2,1)} %slice_bitcast_fusion), channel_id=1, source_target_pairs={{0,1},{1,0},{2,3},{3,2},{4,5},{5,4},{6,7},{7,6},{8,9},{9,8},{10,11... | collective-permute-start | bytes 1572872 | tf_op jit(solution)/shard_map/ppermute | solution.py:261
  223.0 16.8 %copy-start.25 = (bf16[2,2,128,1024]{3,2,0,1:T(8,128)(2,1)S(1)}, bf16[2,2,128,1024]{3,2,0,1:T(8,128)(2,1)}, u32[]{:S(2)}) copy-start(bf16[2,2,128,1024]{3,2,0,1:T(8,128)(2,1)} %copy-done.24) | copy-start | bytes 3145732
  235.1 16.8 %all-to-all-start.5 = ((f32[8,8,1536]{2,1,0:T(8,128)}), f32[8,8,1536]{2,1,0:T(8,128)S(1)}, u32[]{:S(2)}, u32[]{:S(2)}) async-start(f32[8,8,1536]{2,1,0:T(8,128)} %broadcast_in_dim.5), calls=%async_computation.5 | async-start | bytes 786432 | tf_op jit(solution)/shard_map/all_to_all | solution.py:276
Sparse Core Ops, SparseCore 0:
  10.4 66.7 all-gather.1

commit v2 on v1

v2 whole, which is shorter than its diff:
```python
import functools

import jax
import jax.numpy as jnp
from jax import lax
from jax.experimental import pallas as pl
from jax.experimental.pallas import tpu as pltpu
from jax.sharding import PartitionSpec as P

HD = 64
VMEM_BYTES = 60 * 2**20
F32 = jnp.float32
BF16 = jnp.bfloat16
NT = (((1,), (1,)), ((), ()))
TN = (((0,), (0,)), ((), ()))


def prepare_kernel(layer_ref, maps_ref, wq, wk, wv, table_ref, packed_ref):
    owners, _, share, _ = table_ref.shape
    begin = pl.multiple_of(layer_ref[0] * share, share)
    mine = maps_ref[:, pl.ds(begin, share), :]
    for owner in range(owners):
        table_ref[owner] = mine
    local = wq.shape[1]
    for i, w in enumerate((wq, wk, wv)):
        packed_ref[:, pl.ds(i * local, local)] = w[...]


def prepare(layer, store_maps, wq, wk, wv, owners, share):
    entries, _, channels = store_maps.shape
    rows, local = wq.shape
    vmem = pl.BlockSpec(memory_space=pltpu.VMEM)
    return pl.pallas_call(
        prepare_kernel,
        out_shape=[
            jax.ShapeDtypeStruct((owners, entries, share, channels), BF16),
            jax.ShapeDtypeStruct((rows, 3 * local), BF16),
        ],
        in_specs=[pl.BlockSpec(memory_space=pltpu.SMEM)] + [vmem] * 4,
        out_specs=[vmem] * 2,
        compiler_params=pltpu.CompilerParams(vmem_limit_bytes=16 * 2**20),
        name="prepare",
    )(layer.reshape(1).astype(jnp.int32), store_maps, wq, wk, wv)


def pick_kernel(where_ref, table_ref, *outs):
    layers, per = outs[0].shape[:2]
    for number, out in enumerate(outs):
        for layer in range(layers):
            for item in range(per):
                place = where_ref[(number * layers + layer) * per + item]
                out[layer, item] = table_ref[place]


def pick(table, where, chunks, layers, per):
    rows, channels = table.shape[1:]
    vmem = pl.BlockSpec(memory_space=pltpu.VMEM)
    return pl.pallas_call(
        pick_kernel,
        out_shape=[jax.ShapeDtypeStruct((layers, per, rows, channels), table.dtype)] * chunks,
        in_specs=[pl.BlockSpec(memory_space=pltpu.SMEM), vmem],
        out_specs=[vmem] * chunks,
        compiler_params=pltpu.CompilerParams(vmem_limit_bytes=16 * 2**20),
        name="pick",
    )(where, table)


def attention_kernel(has_before, *refs):
    xo, xt, uo, ut, no, nt, wq, wk, wv = refs[:9]
    before = refs[9] if has_before else None
    gqo, gqt, sums, q_s, k_s, v_s, gq_s, gkv_s = refs[9 + has_before :]
    prompts, half, channels = xo.shape
    layers, _, rows, _ = no.shape
    part = layers * rows
    width = wq.shape[1]
    tokens, maps = (xo, xt), (no, nt)
    for i in range(2):
        x = tokens[i][...].reshape(prompts * half, channels)
        n = maps[i][...].reshape(prompts * part, channels)
        q = jnp.dot(x, wq[...], preferred_element_type=F32).astype(BF16)
        k = jnp.dot(n, wk[...], preferred_element_type=F32).astype(BF16)
        v = jnp.dot(n, wv[...], preferred_element_type=F32).astype(BF16)
        q_s[i] = q.reshape(prompts, half, width)
        k_s[i] = k.reshape(layers, prompts, rows, width)
        v_s[i] = v.reshape(layers, prompts, rows, width)
    scale = HD ** (-0.5)
    lane = lax.broadcasted_iota(jnp.int32, (1, 2 * HD), 1)
    first = lane < HD

    def both(array):
        return jnp.concatenate([array[0], array[1]], axis=0)

    for p in range(prompts):
        for pair in range(width // (2 * HD)):
            cols = pl.ds(pair * 2 * HD, 2 * HD)
            kp = both([k_s[i, :, p, :, cols].reshape(part, 2 * HD) for i in range(2)])
            vp = both([v_s[i, :, p, :, cols].reshape(part, 2 * HD) for i in range(2)])
            qp = both([q_s[i, p, :, cols] for i in range(2)])
            up = both([uo[p, :, cols], ut[p, :, cols]])
            kt = kp.T
            grad_k = grad_v = None
            grad_q = []
            for side in range(2):
                keep = jnp.where(first if side == 0 else jnp.logical_not(first), 1.0, 0.0)
                qm = qp * (keep * scale).astype(BF16)
                um = up * keep.astype(BF16)
                s = lax.dot_general(kp, qm, NT, preferred_element_type=F32)
                dw = lax.dot_general(vp, um, NT, preferred_element_type=F32)
                e = jnp.exp(s - jnp.max(s, axis=0, keepdims=True))
                inverse = 1.0 / jnp.sum(e, axis=0, keepdims=True)
                att = e * inverse
                row = jnp.sum(e * dw, axis=0, keepdims=True) * inverse
                gv_part = jnp.dot(att.astype(BF16), um, preferred_element_type=F32)
                ds = (att * (dw - row)).astype(BF16)
                gk_part = jnp.dot(ds, qm, preferred_element_type=F32)
                grad_q.append(
                    jnp.dot(kt[side * HD : (side + 1) * HD], ds, preferred_element_type=F32)
                )
                grad_v = gv_part if grad_v is None else grad_v + gv_part
                grad_k = gk_part if grad_k is None else grad_k + gk_part
            gq = (both(grad_q) * scale).T.astype(BF16)
            gk, gv = grad_k.astype(BF16), grad_v.astype(BF16)
            more = pl.ds(width + pair * 2 * HD, 2 * HD)
            for i, out in enumerate((gqo, gqt)):
                out[p, :, cols] = gq[i * half : (i + 1) * half]
                gq_s[i, p, :, cols] = gq[i * half : (i + 1) * half]
                here = slice(i * part, (i + 1) * part)
                gkv_s[i, :, p, :, cols] = gk[here].reshape(layers, rows, 2 * HD)
                gkv_s[i, :, p, :, more] = gv[here].reshape(layers, rows, 2 * HD)
    gq_all = gq_s[...].reshape(2 * prompts * half, width)
    gkv_all = gkv_s[...].reshape(2 * prompts * part, 2 * width)
    block = 256
    for begin in range(0, channels, block):
        at = pl.ds(begin, block)
        x = both([t[:, :, at].reshape(prompts * half, block) for t in tokens])
        n = both([t[:, :, :, at].reshape(prompts * part, block) for t in maps])
        dq = lax.dot_general(x, gq_all, TN, preferred_element_type=F32)
        dkv = lax.dot_general(n, gkv_all, TN, preferred_element_type=F32)
        for i, total in enumerate((dq, dkv[:, :width], dkv[:, width:])):
            if before is None:
                sums[i, at] = total
            else:
                total = (total + before[i, at]).astype(BF16)
                share = sums.shape[2]
                own = begin // share
                sums[own : own + block // share, i] = total.reshape(
                    block // share, share, width
                )


def attention(xo, xt, uo, ut, no, nt, weights, before, chunk, owners):
    layers, prompts, rows, channels = no.shape
    half = xo.shape[1]
    part = layers * rows
    local = weights.shape[1] // 3
    step = min(local, 4 * HD)
    steps = local // step
    token_spec = pl.BlockSpec((prompts, half, channels), lambda c: (chunk, 0, 0))
    up_spec = pl.BlockSpec((prompts, half, step), lambda c: (chunk, 0, c))
    map_spec = pl.BlockSpec(no.shape, lambda c: (0, 0, 0, 0))
    w_specs = [
        pl.BlockSpec((channels, step), lambda c, i=i: (0, c + i * steps)) for i in range(3)
    ]
    grad_spec = pl.BlockSpec((prompts, half, step), lambda c: (0, 0, c))
    wide_spec = pl.BlockSpec((3, channels, step), lambda c: (0, 0, c))
    has_before = before is not None
    if has_before:
        share = channels // owners
        sum_shape = jax.ShapeDtypeStruct((owners, 3, share, local), BF16)
        sum_spec = pl.BlockSpec((owners, 3, share, step), lambda c: (0, 0, 0, c))
    else:
        sum_shape = jax.ShapeDtypeStruct((3, channels, local), F32)
        sum_spec = wide_spec
    return pl.pallas_call(
        functools.partial(attention_kernel, has_before),
        grid=(steps,),
        out_shape=[jax.ShapeDtypeStruct((prompts, half, local), BF16)] * 2 + [sum_shape],
        in_specs=[token_spec, token_spec, up_spec, up_spec, map_spec, map_spec]
        + w_specs
        + [wide_spec] * has_before,
        out_specs=[grad_spec, grad_spec, sum_spec],
        scratch_shapes=[
            pltpu.VMEM((2, prompts, half, step), BF16),
            pltpu.VMEM((2, layers, prompts, rows, step), BF16),
            pltpu.VMEM((2, layers, prompts, rows, step), BF16),
            pltpu.VMEM((2, prompts, half, step), BF16),
            pltpu.VMEM((2, layers, prompts, rows, 2 * step), BF16),
        ],
        compiler_params=pltpu.CompilerParams(vmem_limit_bytes=VMEM_BYTES),
        cost_estimate=pl.CostEstimate(
            flops=prompts * 2 * 2 * (2 * half + 4 * part) * channels * local,
            bytes_accessed=16 * 2**20,
            transcendentals=prompts * 2 * half * 2 * part * (local // HD),
        ),
        name="attention",
    )(xo, xt, uo, ut, no, nt, weights, weights, weights, *([before] if has_before else []))


def hold(array, after):
    anywhere = pl.BlockSpec(memory_space=pl.ANY)
    return pl.pallas_call(
        lambda array_ref, after_ref, out_ref: None,
        out_shape=jax.ShapeDtypeStruct(array.shape, array.dtype),
        in_specs=[anywhere, anywhere],
        out_specs=anywhere,
        input_output_aliases={0: 0},
        name="hold",
    )(array, after)


def per_device(
    features,
    store_maps,
    neighbour_owner,
    neighbour_slot,
    query_weight,
    key_weight,
    value_weight,
    grad_context,
):
    prompts, half, channels = features.shape
    entries = store_maps.shape[0]
    owners = lax.axis_size("store")
    layers = lax.axis_size("batch")
    local = query_weight.shape[1]
    layer, core = lax.axis_index("batch"), lax.axis_index("space")
    swap = [(0, 1), (1, 0)]

    share = half // layers
    spread, packed = prepare(
        layer, store_maps, query_weight, key_weight, value_weight, owners, share
    )
    table = lax.all_to_all(
        spread, "store", split_axis=0, concat_axis=0, tiled=True
    ).reshape(owners * entries, share, channels)

    listed = (neighbour_owner * entries + neighbour_slot).reshape(1, -1)
    reach = 1
    while reach < layers:
        moved = lax.ppermute(
            listed, "batch", [(z, (z + reach) % layers) for z in range(layers)]
        )
        listed = jnp.concatenate([listed, moved], axis=0)
        reach *= 2
    place = jnp.roll(listed[::-1], layer + 1, axis=0)
    chunks = 2
    per_chunk = prompts // chunks
    per = 2 * per_chunk
    order = place.reshape(layers, chunks, per).transpose(1, 0, 2).reshape(-1)
    picked = pick(table, order, chunks, layers, per)

    weights = lax.all_gather(packed, "store", axis=0, tiled=True)
    full_query = weights[:, :local]

    x_other = lax.ppermute(features, "space", swap)
    u_own = lax.dynamic_slice_in_dim(grad_context, core * local, local, axis=2)
    u_send = lax.dynamic_slice_in_dim(grad_context, (1 - core) * local, local, axis=2)
    u_other = lax.ppermute(u_send, "space", swap)

    sums = gq = None
    features_out = []
    for chunk in range(chunks):
        n_own = lax.all_to_all(
            picked[chunk], "batch", split_axis=0, concat_axis=0, tiled=True
        ).reshape(layers, per_chunk, 2 * share, channels)
        if gq is not None:
            n_own = hold(n_own, gq)
        n_other = lax.ppermute(n_own, "space", swap)
        gq, gq_other, sums = attention(
            features, x_other, u_own, u_other, n_own, n_other, weights, sums, chunk, owners
        )

        def rows_of(grad):
            product = lax.dot_general(
                grad, full_query, (((2,), (1,)), ((), ())), preferred_element_type=F32
            )
            return lax.reduce_precision(product, exponent_bits=8, mantissa_bits=7)

        received = lax.ppermute(rows_of(gq_other).astype(BF16), "space", swap)
        features_out.append((rows_of(gq) + received.astype(F32)).astype(BF16))
    grad_features = jnp.concatenate(features_out, axis=0)

    row_share = channels // owners
    came = lax.all_to_all(sums, "store", split_axis=0, concat_axis=0, tiled=True)
    layer_sum = jnp.sum(came.astype(F32), axis=0)
    share = row_share // layers
    pieces = layer_sum.reshape(3, layers, share, local).transpose(1, 0, 2, 3)
    crossed = lax.all_to_all(pieces, "batch", split_axis=0, concat_axis=0, tiled=True)
    summed = jnp.sum(crossed, axis=0, keepdims=True)
    totals = lax.all_to_all(
        jnp.broadcast_to(summed, pieces.shape), "batch", split_axis=0, concat_axis=0, tiled=True
    )
    grads = [totals[:, i].reshape(row_share, local) for i in range(3)]
    return (grad_features, *grads)


def solution(mesh):
    in_specs = (
        P(("store", "batch"), "space", None),
        P("store", "space", None),
        P(("store", "batch"), None),
        P(("store", "batch"), None),
        P("store", "space"),
        P("store", "space"),
        P("store", "space"),
        P(("store", "batch"), "space", None),
    )
    out_specs = (
        P(("store", "batch"), "space", None),
        P("store", "space"),
        P("store", "space"),
        P("store", "space"),
    )
    return jax.shard_map(
        per_device, mesh=mesh, in_specs=in_specs, out_specs=out_specs, check_vma=False
    )
```

time: 264 us -> 240 us (0.909); the launches traced: 259 us -> 239 us
  blocking collectives: 37.4 us -> 81.3 us
  waiting for transfers between devices: 87.5 us -> 47.6 us
  local copies, waits for them, and re-layouts: 27.4 us -> 14.5 us
  starting transfers between devices: 36.1 us -> 28.7 us
  other arithmetic: 8.39 us -> 2.26 us
  matrix products: 3.92 us -> 7.63 us
    all_to_all x0 -> x1, blocking collectives: none -> 43.7 us  [per_device(): lax.all_to_all(sums, 'store', split_axis=0, concat_axis=0, tiled=True)]
    all_to_all x2 -> x1, waiting for transfers between devices: 50.2 us -> 9.15 us  [per_device(): lax.all_to_all(spread, 'store', split_axis=0, concat_axis=0, tiled=True)]
    unnamed x56 -> x26, local copies, waits for them, and re-layouts: 20 us -> 8.83 us
    all_to_all x2 -> x1, starting transfers between devices: 14.5 us -> 7.48 us  [per_device(): lax.all_to_all(spread, 'store', split_axis=0, concat_axis=0, tiled=True)]
    dot_general x2 -> x4, matrix products: 3.92 us -> 7.63 us  [rows_of(): lax.dot_general(grad, full_query, (((2,), (1,)), ((), ())), preferred_ele...]
    ppermute x2, waiting for transfers between devices: 0.01 us -> 2.86 us  [per_device(): n_other = lax.ppermute(n_own, 'space', swap)]
    pallas_call x4 -> x3, Pallas kernels: 43.7 us -> 41.5 us  [the longest x2 40.6 us: attention(): pl.pallas_call(functools.partial(attention_kernel, has_before), grid=(ste...]
  transfers between devices with their start and end apart: 15 -> 14, of which waited for: 8 -> 9; matrix products, arithmetic and copies ran while one was open for 7% -> 6% of each run, Pallas kernels for 9% -> 9%
where the time goes in v2:
time: 240 us; the launch traced here: 239 us
  blocking collectives  81.3 us (34%)
  waiting for transfers between devices  47.6 us (20%)
  Pallas kernels  43.1 us (18%)
  starting transfers between devices  28.7 us (12%)
  local copies, waits for them, and re-layouts  14.5 us (6%)
  between operations  14.2 us (6%)
  matrix products  7.63 us (3%)
    all_to_all x1, blocking collectives, per_device(): lax.all_to_all(sums, 'store', split_axis=0, concat_axis=0, tiled=True)  43.7 us
    pallas_call x2, Pallas kernels, attention(): pl.pallas_call(functools.partial(attention_kernel, has_before), grid=(ste...  40.6 us
    all_to_all x1, blocking collectives, per_device(): lax.all_to_all(picked[chunk], 'batch', split_axis=0, concat_axis=0, tiled...  37.6 us
    ppermute x3, waiting for transfers between devices, per_device(): lax.ppermute(listed, 'batch', [(z, (z + reach) % layers) for z in range(l...  14 us
    all_to_all x1, waiting for transfers between devices, per_device(): lax.all_to_all(pieces, 'batch', split_axis=0, concat_axis=0, tiled=True)  9.49 us
    all_to_all x1, waiting for transfers between devices, per_device(): lax.all_to_all(spread, 'store', split_axis=0, concat_axis=0, tiled=True)  9.15 us
    all_to_all x1, waiting for transfers between devices, per_device(): lax.all_to_all(jnp.broadcast_to(summed, pieces.shape), 'batch', split_axi...  9.08 us
    unnamed x26, local copies, waits for them, and re-layouts  8.83 us
  transfers between devices with their start and end apart: 14, of which 9 were waited for; matrix products, arithmetic and copies ran while one was open for 6% of the time, Pallas kernels for 9%

profile of v2, /device:TPU:4, one launch (start us, length us, event | category | flops | bytes accessed | tf_op | source)
XLA Modules:
  0.0 239.4 jit_solution(12443353712449742803)
XLA Ops:
  7.2 1.2 copy-done.1
  8.5 0.8 copy-done.2
  9.3 0.8 copy-done.3
  10.1 0.8 copy-done.4
  11.0 0.9 prepare.1
  11.9 1.4 copy-done
  13.3 7.5 %all-to-all-start = ((bf16[16,4,16,1024]{3,2,1,0:T(8,128)(2,1)}), bf16[16,4,16,1024]{3,2,1,0:T(8,128)(2,1)S(1)}, u32[]{:S(2)}, u32[]{:S(2)}) async-start(bf16[16,4,16,1024]{3,2,1,0:T(8,128)(2,1)} %copy-done), calls=%async_computation | async-start | bytes 4194304 | tf_op jit(solution)/shard_map/all_to_all | solution.py:233
  20.8 0.1 copy.22
  20.9 1.9 collective-permute-start.2
  22.9 5.5 %collective-permute-done.2 = s32[1,8]{1,0:T(1,128)S(1)} collective-permute-done((s32[1,8]{1,0:T(1,128)S(1)}, s32[1,8]{1,0:T(1,128)S(1)}, u32[]{:S(2)}, u32[]{:S(2)}) %collective-permute-start.2) | collective-permute-done | bytes 64 | tf_op jit(solution)/shard_map/ppermute | solution.py:240
  28.4 5.7 %collective-permute-done.3 = s32[2,8]{1,0:T(2,128)S(1)} collective-permute-done((s32[2,8]{1,0:T(2,128)S(1)}, s32[2,8]{1,0:T(2,128)S(1)}, u32[]{:S(2)}, u32[]{:S(2)}) %collective-permute-start.3) | collective-permute-done | bytes 96 | tf_op jit(solution)/shard_map/ppermute | solution.py:240
  34.1 4.7 %collective-permute-start.4 = (s32[4,8]{1,0:T(4,128)S(1)}, s32[4,8]{1,0:T(4,128)S(1)}, u32[]{:S(2)}, u32[]{:S(2)}) collective-permute-start(s32[4,8]{1,0:T(4,128)S(1)} %pad_add_fusion.1), channel_id=1, source_target_pairs={{0,8},{2,10},{4,12},{6,14},{8,0},{10,2},{12,4},{14,6},{1,9},{3,11}... | collective-permute-start | bytes 392 | tf_op jit(solution)/shard_map/ppermute | solution.py:240
  38.7 2.9 %collective-permute-done.4 = s32[4,8]{1,0:T(4,128)S(1)} collective-permute-done((s32[4,8]{1,0:T(4,128)S(1)}, s32[4,8]{1,0:T(4,128)S(1)}, u32[]{:S(2)}, u32[]{:S(2)}) %collective-permute-start.4) | collective-permute-done | bytes 160 | tf_op jit(solution)/shard_map/ppermute | solution.py:240
  41.8 0.1 copy.24
  41.9 0.1 reshape.35.where_ref
  42.0 9.2 %all-to-all-done = bf16[16,4,16,1024]{3,2,1,0:T(8,128)(2,1)S(1)} async-done(((bf16[16,4,16,1024]{3,2,1,0:T(8,128)(2,1)}), bf16[16,4,16,1024]{3,2,1,0:T(8,128)(2,1)S(1)}, u32[]{:S(2)}, u32[]{:S(2)}) %all-to-all-start) | async-done | bytes 2097184 | tf_op jit(solution)/shard_map/all_to_all | solution.py:233
  51.1 1.7 pick.1
  52.8 37.6 %all_to_all.30 = bf16[8,4,16,1024]{3,2,1,0:T(8,128)(2,1)} all-to-all(bf16[8,4,16,1024]{3,2,1,0:T(8,128)(2,1)S(1)} %get-tuple-element.15), channel_id=1, replica_groups=mesh['store'=16,'batch'=8,'space'=2] {'batch'}, dimensions={0} | all-to-all | bytes 2097152 | tf_op jit(solution)/shard_map/all_to_all | solution.py:263
  90.4 3.6 %all-to-all-start.2 = ((bf16[8,4,16,1024]{3,2,1,0:T(8,128)(2,1)}), bf16[8,4,16,1024]{3,2,1,0:T(8,128)(2,1)S(1)}, u32[]{:S(2)}, u32[]{:S(2)}) async-start(bf16[8,4,16,1024]{3,2,1,0:T(8,128)(2,1)} %get-tuple-element.19), calls=%async_computation.2 | async-start | bytes 2097152 | tf_op jit(solution)/shard_map/all_to_all | solution.py:263
  93.9 0.1 collective-permute-start
  94.0 0.5 collective-permute-start.5
  94.5 2.1 constant_dynamic-slice_fusion
  96.7 0.1 collective-permute-start.1
  96.8 2.2 collective-permute-done.1.refs_3_
  98.9 0.8 copy-done.10
  99.7 1.0 copy-done.8
  100.7 20.0 %attention.2 = (bf16[2,128,512]{2,1,0:T(8,128)(2,1)}, bf16[2,128,512]{2,1,0:T(8,128)(2,1)}, f32[3,1024,512]{2,1,0:T(8,128)}) custom-call(bf16[4,128,1024]{2,1,0:T(8,128)(2,1)} %refs_0_.3, bf16[4,128,1024]{2,1,0:T(8,128)(2,1)} %copy-done.8, bf16[4,128,512]{2,1,0:T(8,128)(2,1)} %get-tuple-element.25.refs_2_, bf16[4,128,512]{2,1,0:T(8,128)(2,1)} %copy-done.10, ...), custom_call_target="tpu_custom_call" | custom-call | flops 5368709120 | bytes 16777216 | tf_op jit(solution)/shard_map/attention/pallas_call | solution.py:174
  120.7 0.8 all-to-all-done.2
  121.5 1.0 copy-done.6
  122.5 2.9 %collective-permute-done.7.refs_5_ = bf16[8,2,32,1024]{3,2,1,0:T(8,128)(2,1)S(1)} collective-permute-done((bf16[8,2,32,1024]{3,2,1,0:T(8,128)(2,1)}, bf16[8,2,32,1024]{3,2,1,0:T(8,128)(2,1)S(1)}, u32[]{:S(2)}, u32[]{:S(2)}) %collective-permute-start.7) | collective-permute-done | bytes 1048608 | tf_op jit(solution)/shard_map/ppermute | solution.py:268
  125.3 1.0 copy-done.9
  126.3 20.5 %attention.3 = (bf16[2,128,512]{2,1,0:T(8,128)(2,1)}, bf16[2,128,512]{2,1,0:T(8,128)(2,1)}, bf16[16,3,64,512]{3,2,1,0:T(8,128)(2,1)}) custom-call(bf16[4,128,1024]{2,1,0:T(8,128)(2,1)} %refs_0_.3, bf16[4,128,1024]{2,1,0:T(8,128)(2,1)} %copy-done.8, bf16[4,128,512]{2,1,0:T(8,128)(2,1)} %get-tuple-element.25.refs_2_, bf16[4,128,512]{2,1,0:T(8,128)(2,1)} %copy-done.10, ...), custom_call_target="tpu_custom_call" | custom-call | flops 5368709120 | bytes 16777216 | tf_op jit(solution)/shard_map/attention/pallas_call | solution.py:174
  146.9 43.7 %all_to_all.31 = bf16[16,3,64,512]{3,2,1,0:T(8,128)(2,1)S(1)} all-to-all(bf16[16,3,64,512]{3,2,1,0:T(8,128)(2,1)} %get-tuple-element.23), channel_id=1, replica_groups=mesh['store'=16,'batch'=8,'space'=2] {'store'}, dimensions={0} | all-to-all | bytes 6291456 | tf_op jit(solution)/shard_map/all_to_all | solution.py:284
  190.6 0.5 convert_reduce_fusion
  191.1 0.8 copy.25
  191.9 6.4 %all-to-all-start.4 = ((f32[8,3,8,512]{3,2,1,0:T(8,128)}), f32[8,3,8,512]{3,2,1,0:T(8,128)S(1)}, u32[]{:S(2)}, u32[]{:S(2)}) async-start(f32[8,3,8,512]{3,2,1,0:T(8,128)} %copy.25), calls=%async_computation.4 | async-start | bytes 786432 | tf_op jit(solution)/shard_map/all_to_all | solution.py:288
  198.2 2.2 fusion.2
  200.5 2.2 fusion.3
  202.7 0.5 collective-permute-start.8
  203.2 9.5 %all-to-all-done.4 = f32[8,3,8,512]{3,2,1,0:T(8,128)S(1)} async-done(((f32[8,3,8,512]{3,2,1,0:T(8,128)}), f32[8,3,8,512]{3,2,1,0:T(8,128)S(1)}, u32[]{:S(2)}, u32[]{:S(2)}) %all-to-all-start.4) | async-done | bytes 393248 | tf_op jit(solution)/shard_map/all_to_all | solution.py:288
  212.7 0.6 reduce_sum.19
  213.3 1.6 broadcast_in_dim.2
  214.9 3.5 %all-to-all-start.5 = ((f32[8,3,8,512]{3,2,1,0:T(8,128)}), f32[8,3,8,512]{3,2,1,0:T(8,128)S(1)}, u32[]{:S(2)}, u32[]{:S(2)}) async-start(f32[8,3,8,512]{3,2,1,0:T(8,128)} %broadcast_in_dim.2), calls=%async_computation.5 | async-start | bytes 786432 | tf_op jit(solution)/shard_map/all_to_all | solution.py:290
  218.4 1.6 fusion.5
  220.0 1.6 fusion.4
  221.6 1.1 pad_maximum_fusion
  222.7 9.1 %all-to-all-done.5 = f32[8,3,8,512]{3,2,1,0:T(8,128)S(1)} async-done(((f32[8,3,8,512]{3,2,1,0:T(8,128)}), f32[8,3,8,512]{3,2,1,0:T(8,128)S(1)}, u32[]{:S(2)}, u32[]{:S(2)}) %all-to-all-start.5) | async-done | bytes 393248 | tf_op jit(solution)/shard_map/all_to_all | solution.py:290
  231.8 0.8 slice_bitcast_fusion.5
  (36 shorter events, 0.4 us)
Async XLA Ops:
  7.2 13.6 %copy-start.11 = (s32[4,2]{0,1:T(2,128)S(1)}, s32[4,2]{0,1:T(2,128)}, u32[]{:S(2)}) copy-start(s32[4,2]{0,1:T(2,128)} %param.11) | copy-start | bytes 100
  7.2 13.6 %copy-start.12 = (s32[4,2]{0,1:T(2,128)S(1)}, s32[4,2]{0,1:T(2,128)}, u32[]{:S(2)}) copy-start(s32[4,2]{0,1:T(2,128)} %param.10) | copy-start | bytes 100
  7.2 92.6 %all-gather.2.cloned.1.call-start = ((), (), s32[]{:S(2)}) async-start(), calls=%async_computation.6 | async-start | bytes 3342336 | tf_op jit(solution)/shard_map/all_gather | solution.py:252
  7.2 1.2 copy-start.1
  8.5 0.8 copy-start.2
  9.3 0.8 copy-start.3
  10.1 0.8 copy-start.4
  11.9 1.4 copy-start
  13.3 37.8 %all-to-all-start = ((bf16[16,4,16,1024]{3,2,1,0:T(8,128)(2,1)}), bf16[16,4,16,1024]{3,2,1,0:T(8,128)(2,1)S(1)}, u32[]{:S(2)}, u32[]{:S(2)}) async-start(bf16[16,4,16,1024]{3,2,1,0:T(8,128)(2,1)} %copy-done), calls=%async_computation | async-start | bytes 4194304 | tf_op jit(solution)/shard_map/all_to_all | solution.py:233
  20.9 7.4 %collective-permute-start.2 = (s32[1,8]{1,0:T(1,128)S(1)}, s32[1,8]{1,0:T(1,128)S(1)}, u32[]{:S(2)}, u32[]{:S(2)}) collective-permute-start(s32[1,8]{1,0:T(1,128)S(1)} %reshape.33), channel_id=1, source_target_pairs={{0,2},{2,4},{4,6},{6,8},{8,10},{10,12},{12,14},{14,0},{1,3},{3,5},... | collective-permute-start | bytes 104 | tf_op jit(solution)/shard_map/ppermute | solution.py:240
  28.3 5.8 %collective-permute-start.3 = (s32[2,8]{1,0:T(2,128)S(1)}, s32[2,8]{1,0:T(2,128)S(1)}, u32[]{:S(2)}, u32[]{:S(2)}) collective-permute-start(s32[2,8]{1,0:T(2,128)S(1)} %pad_add_fusion.2), channel_id=1, source_target_pairs={{0,4},{2,6},{4,8},{6,10},{8,12},{10,14},{12,0},{14,2},{1,5},{3,7},... | collective-permute-start | bytes 200 | tf_op jit(solution)/shard_map/ppermute | solution.py:240
  34.1 7.6 %collective-permute-start.4 = (s32[4,8]{1,0:T(4,128)S(1)}, s32[4,8]{1,0:T(4,128)S(1)}, u32[]{:S(2)}, u32[]{:S(2)}) collective-permute-start(s32[4,8]{1,0:T(4,128)S(1)} %pad_add_fusion.1), channel_id=1, source_target_pairs={{0,8},{2,10},{4,12},{6,14},{8,0},{10,2},{12,4},{14,6},{1,9},{3,11}... | collective-permute-start | bytes 392 | tf_op jit(solution)/shard_map/ppermute | solution.py:240
  51.1 42.8 %copy-start.7 = (bf16[4,128,1024]{2,1,0:T(8,128)(2,1)S(1)}, bf16[4,128,1024]{2,1,0:T(8,128)(2,1)}, u32[]{:S(2)}) copy-start(bf16[4,128,1024]{2,1,0:T(8,128)(2,1)} %refs_0_.3) | copy-start | bytes 3145732
  90.4 31.1 %all-to-all-start.2 = ((bf16[8,4,16,1024]{3,2,1,0:T(8,128)(2,1)}), bf16[8,4,16,1024]{3,2,1,0:T(8,128)(2,1)S(1)}, u32[]{:S(2)}, u32[]{:S(2)}) async-start(bf16[8,4,16,1024]{3,2,1,0:T(8,128)(2,1)} %get-tuple-element.19), calls=%async_computation.2 | async-start | bytes 2097152 | tf_op jit(solution)/shard_map/all_to_all | solution.py:263
  93.9 5.0 %collective-permute-start = (bf16[4,128,1024]{2,1,0:T(8,128)(2,1)S(1)}, bf16[4,128,1024]{2,1,0:T(8,128)(2,1)S(1)}, u32[]{:S(2)}, u32[]{:S(2)}) collective-permute-start(bf16[4,128,1024]{2,1,0:T(8,128)(2,1)S(1)} %copy-done.7), channel_id=1, source_target_pairs={{0,1},{1,0},{2,3},{3,2},{4,5},{5,4},{6,7},{7,6},{8,9},{9,8},{10,11... | collective-permute-start | bytes 3145736 | tf_op jit(solution)/shard_map/ppermute | solution.py:255
  94.0 5.7 %collective-permute-start.5 = (bf16[8,2,32,1024]{3,2,1,0:T(8,128)(2,1)}, bf16[8,2,32,1024]{3,2,1,0:T(8,128)(2,1)}, u32[]{:S(2)}, u32[]{:S(2)}) collective-permute-start(bf16[8,2,32,1024]{3,2,1,0:T(8,128)(2,1)} %bitcast.29), channel_id=1, source_target_pairs={{0,1},{1,0},{2,3},{3,2},{4,5},{5,4},{6,7},{7,6},{8,9},{9,8},{10,11... | collective-permute-start | bytes 3145736 | tf_op jit(solution)/shard_map/ppermute | solution.py:268
  96.7 2.3 collective-permute-start.1
  98.9 0.8 copy-start.10
  99.7 1.0 copy-start.8
  121.5 1.0 copy-start.6
  122.5 2.9 %collective-permute-start.7 = (bf16[8,2,32,1024]{3,2,1,0:T(8,128)(2,1)}, bf16[8,2,32,1024]{3,2,1,0:T(8,128)(2,1)S(1)}, u32[]{:S(2)}, u32[]{:S(2)}) collective-permute-start(bf16[8,2,32,1024]{3,2,1,0:T(8,128)(2,1)} %hold.1.refs_4_), channel_id=1, source_target_pairs={{0,1},{1,0},{2,3},{3,2},{4,5},{5,4},{6,7},{7,6},{8,9},{9,8},{10,11... | collective-permute-start | bytes 3145736 | tf_op jit(solution)/shard_map/ppermute | solution.py:268
  125.3 1.0 copy-start.9
  190.6 7.7 %copy-start.5 = (bf16[1024,1536]{1,0:T(8,128)(2,1)S(1)}, bf16[1024,1536]{1,0:T(8,128)(2,1)}, u32[]{:S(2)}) copy-start(bf16[1024,1536]{1,0:T(8,128)(2,1)} %all-gather.2.cloned.1.call-done.refs_6_.refs_7_.refs_8_) | copy-start | bytes 9437188
  191.9 20.8 %all-to-all-start.4 = ((f32[8,3,8,512]{3,2,1,0:T(8,128)}), f32[8,3,8,512]{3,2,1,0:T(8,128)S(1)}, u32[]{:S(2)}, u32[]{:S(2)}) async-start(f32[8,3,8,512]{3,2,1,0:T(8,128)} %copy.25), calls=%async_computation.4 | async-start | bytes 786432 | tf_op jit(solution)/shard_map/all_to_all | solution.py:288
  200.5 17.9 %collective-permute-start.6 = (bf16[2,128,1024]{2,1,0:T(8,128)(2,1)}, bf16[2,128,1024]{2,1,0:T(8,128)(2,1)}, u32[]{:S(2)}, u32[]{:S(2)}) collective-permute-start(bf16[2,128,1024]{2,1,0:T(8,128)(2,1)} %fusion.2), channel_id=1, source_target_pairs={{0,1},{1,0},{2,3},{3,2},{4,5},{5,4},{6,7},{7,6},{8,9},{9,8},{10,11... | collective-permute-start | bytes 1572872 | tf_op jit(solution)/shard_map/ppermute | solution.py:279
  202.7 17.3 %collective-permute-start.8 = (bf16[2,128,1024]{2,1,0:T(8,128)(2,1)}, bf16[2,128,1024]{2,1,0:T(8,128)(2,1)}, u32[]{:S(2)}, u32[]{:S(2)}) collective-permute-start(bf16[2,128,1024]{2,1,0:T(8,128)(2,1)} %fusion.3), channel_id=1, source_target_pairs={{0,1},{1,0},{2,3},{3,2},{4,5},{5,4},{6,7},{7,6},{8,9},{9,8},{10,11... | collective-permute-start | bytes 1572872 | tf_op jit(solution)/shard_map/ppermute | solution.py:279
  214.9 16.8 %all-to-all-start.5 = ((f32[8,3,8,512]{3,2,1,0:T(8,128)}), f32[8,3,8,512]{3,2,1,0:T(8,128)S(1)}, u32[]{:S(2)}, u32[]{:S(2)}) async-start(f32[8,3,8,512]{3,2,1,0:T(8,128)} %broadcast_in_dim.2), calls=%async_computation.5 | async-start | bytes 786432 | tf_op jit(solution)/shard_map/all_to_all | solution.py:290
Sparse Core Ops, SparseCore 0:
  13.4 66.7 all-gather.1

commit v3 on v2

--- a/solution.py
+++ b/solution.py
@@ -13,6 +13,10 @@
 BF16 = jnp.bfloat16
 NT = (((1,), (1,)), ((), ()))
 TN = (((0,), (0,)), ((), ()))
+
+
+def whole(memory):
+    return pl.BlockSpec(memory_space=memory)
 
 
 def prepare_kernel(layer_ref, maps_ref, wq, wk, wv, table_ref, packed_ref):
@@ -38,12 +42,32 @@
         ],
         in_specs=[pl.BlockSpec(memory_space=pltpu.SMEM)] + [vmem] * 4,
         out_specs=[vmem] * 2,
-        compiler_params=pltpu.CompilerParams(vmem_limit_bytes=16 * 2**20),
+        compiler_params=pltpu.CompilerParams(vmem_limit_bytes=VMEM_BYTES),
         name="prepare",
     )(layer.reshape(1).astype(jnp.int32), store_maps, wq, wk, wv)
 
 
-def pick_kernel(where_ref, table_ref, *outs):
+def total_kernel(parts_ref, out_ref):
+    total = parts_ref[0]
+    for i in range(1, parts_ref.shape[0]):
+        total = total + parts_ref[i]
+    for i in range(out_ref.shape[0]):
+        out_ref[i] = total
+
+
+def total_for_all(parts):
+    return pl.pallas_call(
+        total_kernel,
+        out_shape=jax.ShapeDtypeStruct(parts.shape, parts.dtype),
+        in_specs=[whole(pltpu.VMEM)],
+        out_specs=whole(pltpu.VMEM),
+        compiler_params=pltpu.CompilerParams(vmem_limit_bytes=16 * 2**20),
+        name="total",
+    )(parts)
+
+
+def pick_kernel(waits, where_ref, table_ref, *refs):
+    outs = refs[waits:]
     layers, per = outs[0].shape[:2]
     for number, out in enumerate(outs):
         for layer in range(layers):
@@ -52,20 +76,20 @@
                 out[layer, item] = table_ref[place]
 
 
-def pick(table, where, chunks, layers, per):
+def pick(table, where, chunks, layers, per, after):
     rows, channels = table.shape[1:]
     vmem = pl.BlockSpec(memory_space=pltpu.VMEM)
     return pl.pallas_call(
-        pick_kernel,
+        functools.partial(pick_kernel, len(after)),
         out_shape=[jax.ShapeDtypeStruct((layers, per, rows, channels), table.dtype)] * chunks,
-        in_specs=[pl.BlockSpec(memory_space=pltpu.SMEM), vmem],
+        in_specs=[whole(pltpu.SMEM), vmem] + [whole(pl.ANY)] * len(after),
         out_specs=[vmem] * chunks,
         compiler_params=pltpu.CompilerParams(vmem_limit_bytes=16 * 2**20),
         name="pick",
-    )(where, table)
-
-
-def attention_kernel(has_before, *refs):
+    )(where, table, *after)
+
+
+def attention_kernel(has_before, core_ref, *refs):
     xo, xt, uo, ut, no, nt, wq, wk, wv = refs[:9]
     before = refs[9] if has_before else None
     gqo, gqt, sums, q_s, k_s, v_s, gq_s, gkv_s = refs[9 + has_before :]
@@ -148,52 +172,55 @@
                 )
 
 
-def attention(xo, xt, uo, ut, no, nt, weights, before, chunk, owners):
+def attention(core, xo, xt, uo, ut, no, nt, weights, before, chunk, owners):
     layers, prompts, rows, channels = no.shape
     half = xo.shape[1]
     part = layers * rows
     local = weights.shape[1] // 3
     step = min(local, 4 * HD)
     steps = local // step
-    token_spec = pl.BlockSpec((prompts, half, channels), lambda c: (chunk, 0, 0))
-    up_spec = pl.BlockSpec((prompts, half, step), lambda c: (chunk, 0, c))
-    map_spec = pl.BlockSpec(no.shape, lambda c: (0, 0, 0, 0))
+    token_spec = pl.BlockSpec((prompts, half, channels), lambda c, core: (chunk, 0, 0))
+    up_spec = pl.BlockSpec((prompts, half, step), lambda c, core: (chunk, 0, c + core[0] * steps))
+    map_spec = whole(pltpu.VMEM)
     w_specs = [
-        pl.BlockSpec((channels, step), lambda c, i=i: (0, c + i * steps)) for i in range(3)
+        pl.BlockSpec((channels, step), lambda c, core, i=i: (0, c + i * steps)) for i in range(3)
     ]
-    grad_spec = pl.BlockSpec((prompts, half, step), lambda c: (0, 0, c))
-    wide_spec = pl.BlockSpec((3, channels, step), lambda c: (0, 0, c))
+    grad_spec = pl.BlockSpec((prompts, half, step), lambda c, core: (0, 0, c))
+    wide_spec = pl.BlockSpec((3, channels, step), lambda c, core: (0, 0, c))
     has_before = before is not None
     if has_before:
         share = channels // owners
         sum_shape = jax.ShapeDtypeStruct((owners, 3, share, local), BF16)
-        sum_spec = pl.BlockSpec((owners, 3, share, step), lambda c: (0, 0, 0, c))
+        sum_spec = pl.BlockSpec((owners, 3, share, step), lambda c, core: (0, 0, 0, c))
     else:
         sum_shape = jax.ShapeDtypeStruct((3, channels, local), F32)
         sum_spec = wide_spec
     return pl.pallas_call(
         functools.partial(attention_kernel, has_before),
-        grid=(steps,),
         out_shape=[jax.ShapeDtypeStruct((prompts, half, local), BF16)] * 2 + [sum_shape],
-        in_specs=[token_spec, token_spec, up_spec, up_spec, map_spec, map_spec]
-        + w_specs
-        + [wide_spec] * has_before,
-        out_specs=[grad_spec, grad_spec, sum_spec],
-        scratch_shapes=[
-            pltpu.VMEM((2, prompts, half, step), BF16),
-            pltpu.VMEM((2, layers, prompts, rows, step), BF16),
-            pltpu.VMEM((2, layers, prompts, rows, step), BF16),
-            pltpu.VMEM((2, prompts, half, step), BF16),
-            pltpu.VMEM((2, layers, prompts, rows, 2 * step), BF16),
-        ],
-        compiler_params=pltpu.CompilerParams(vmem_limit_bytes=VMEM_BYTES),
+        grid_spec=pltpu.PrefetchScalarGridSpec(
+            num_scalar_prefetch=1,
+            grid=(steps,),
+            in_specs=[token_spec, token_spec, up_spec, up_spec, map_spec, map_spec]
+            + w_specs
+            + [wide_spec] * has_before,
+            out_specs=[grad_spec, grad_spec, sum_spec],
+            scratch_shapes=[
+                pltpu.VMEM((2, prompts, half, step), BF16),
+                pltpu.VMEM((2, layers, prompts, rows, step), BF16),
+                pltpu.VMEM((2, layers, prompts, rows, step), BF16),
+                pltpu.VMEM((2, prompts, half, step), BF16),
+                pltpu.VMEM((2, layers, prompts, rows, 2 * step), BF16),
+            ],
+        ),
+        compiler_params=pltpu.CompilerParams(vmem_limit_bytes=50 * 2**20),
         cost_estimate=pl.CostEstimate(
             flops=prompts * 2 * 2 * (2 * half + 4 * part) * channels * local,
             bytes_accessed=16 * 2**20,
             transcendentals=prompts * 2 * half * 2 * part * (local // HD),
         ),
         name="attention",
-    )(xo, xt, uo, ut, no, nt, weights, weights, weights, *([before] if has_before else []))
+    )(core, xo, xt, uo, ut, no, nt, weights, weights, weights, *([before] if has_before else []))
 
 
 def hold(array, after):
@@ -247,15 +274,12 @@
     per_chunk = prompts // chunks
     per = 2 * per_chunk
     order = place.reshape(layers, chunks, per).transpose(1, 0, 2).reshape(-1)
-    picked = pick(table, order, chunks, layers, per)
+    x_other = lax.ppermute(features, "space", swap)
+    u_other = lax.ppermute(grad_context, "space", swap)
+    picked = pick(table, order, chunks, layers, per, [x_other, u_other])
 
     weights = lax.all_gather(packed, "store", axis=0, tiled=True)
     full_query = weights[:, :local]
-
-    x_other = lax.ppermute(features, "space", swap)
-    u_own = lax.dynamic_slice_in_dim(grad_context, core * local, local, axis=2)
-    u_send = lax.dynamic_slice_in_dim(grad_context, (1 - core) * local, local, axis=2)
-    u_other = lax.ppermute(u_send, "space", swap)
 
     sums = gq = None
     features_out = []
@@ -267,7 +291,9 @@
             n_own = hold(n_own, gq)
         n_other = lax.ppermute(n_own, "space", swap)
         gq, gq_other, sums = attention(
-            features, x_other, u_own, u_other, n_own, n_other, weights, sums, chunk, owners
+            core.reshape(1).astype(jnp.int32),
+            features, x_other, grad_context, u_other, n_own, n_other,
+            weights, sums, chunk, owners,
         )
 
         def rows_of(grad):
@@ -286,9 +312,8 @@
     share = row_share // layers
     pieces = layer_sum.reshape(3, layers, share, local).transpose(1, 0, 2, 3)
     crossed = lax.all_to_all(pieces, "batch", split_axis=0, concat_axis=0, tiled=True)
-    summed = jnp.sum(crossed, axis=0, keepdims=True)
     totals = lax.all_to_all(
-        jnp.broadcast_to(summed, pieces.shape), "batch", split_axis=0, concat_axis=0, tiled=True
+        total_for_all(crossed), "batch", split_axis=0, concat_axis=0, tiled=True
     )
     grads = [totals[:, i].reshape(row_share, local) for i in range(3)]
     return (grad_features, *grads)

time: 240 us -> 231 us (0.963)
  local copies, waits for them, and re-layouts: 14.5 us -> 4.39 us
  waiting for transfers between devices: 47.6 us -> 51 us
    unnamed x26 -> x24, local copies, waits for them, and re-layouts: 8.83 us -> 2.43 us
    ppermute x2, waiting for transfers between devices: 2.86 us -> 5.84 us  [per_device(): n_other = lax.ppermute(n_own, 'space', swap)]
    all_to_all x1, starting transfers between devices: 6.37 us -> 3.53 us  [per_device(): lax.all_to_all(pieces, 'batch', split_axis=0, concat_axis=0, tiled=True)]
    all_to_all x1, waiting for transfers between devices: 0.75 us -> 3.33 us  [per_device(): lax.all_to_all(picked[chunk], 'batch', split_axis=0, concat_axis=0, tiled...]
    pallas_call x3 -> x4, Pallas kernels: 42.2 us -> 41.1 us  [the longest x2 39.6 us: attention(): pl.pallas_call(functools.partial(attention_kernel, has_before), out_shape...]
  transfers between devices with their start and end apart: 14 -> 14, of which waited for: 9 -> 9; matrix products, arithmetic and copies ran while one was open for 6% -> 4% of each run, Pallas kernels for 9% -> 9%
where the time goes in v3:
time: 231 us
  blocking collectives  81.6 us (35%)
  waiting for transfers between devices  51 us (22%)
  Pallas kernels  44 us (19%)
  starting transfers between devices  26.9 us (12%)
  between operations  14.3 us (6%)
  matrix products  6.81 us (3%)
  local copies, waits for them, and re-layouts  4.39 us (2%)
    all_to_all x1, blocking collectives, per_device(): lax.all_to_all(sums, 'store', split_axis=0, concat_axis=0, tiled=True)  43.8 us
    pallas_call x2, Pallas kernels, attention(): pl.pallas_call(functools.partial(attention_kernel, has_before), out_shape...  39.6 us
    all_to_all x1, blocking collectives, per_device(): lax.all_to_all(picked[chunk], 'batch', split_axis=0, concat_axis=0, tiled...  37.8 us
    ppermute x3, waiting for transfers between devices, per_device(): lax.ppermute(listed, 'batch', [(z, (z + reach) % layers) for z in range(l...  14 us
    all_to_all x1, waiting for transfers between devices, per_device(): lax.all_to_all(pieces, 'batch', split_axis=0, concat_axis=0, tiled=True)  10.3 us
    all_to_all x1, waiting for transfers between devices, per_device(): lax.all_to_all(total_for_all(crossed), 'batch', split_axis=0, concat_axis...  8.83 us
    all_to_all x1, waiting for transfers between devices, per_device(): lax.all_to_all(spread, 'store', split_axis=0, concat_axis=0, tiled=True)  8.68 us
    all_to_all x1, starting transfers between devices, per_device(): lax.all_to_all(spread, 'store', split_axis=0, concat_axis=0, tiled=True)  7.46 us
  transfers between devices with their start and end apart: 14, of which 9 were waited for; matrix products, arithmetic and copies ran while one was open for 4% of the time, Pallas kernels for 9%

profile of v3, /device:TPU:4, one launch (start us, length us, event | category | flops | bytes accessed | tf_op | source)
XLA Modules:
  0.0 230.5 jit_solution(5631273674676277412)
XLA Ops:
  7.2 0.0 all-gather.2.cloned.1.call-start
  7.2 2.9 %prepare.1 = (bf16[16,4,16,1024]{3,2,1,0:T(8,128)(2,1)}, bf16[64,1536]{1,0:T(8,128)(2,1)}) custom-call(s32[1]{0:T(128)} %bitcast.3.layer_ref, bf16[4,128,1024]{2,1,0:T(8,128)(2,1)} %maps_ref.1, bf16[64,512]{1,0:T(8,128)(2,1)} %wq.1, bf16[64,512]{1,0:T(8,128)(2,1)} %wk.1, bf16[64,512]{1,0:T(8,128)(2,1)} %wv.1), custom_call_target="tpu_custom_call" | custom-call | tf_op jit(solution)/shard_map/prepare/pallas_call | solution.py:37
  10.1 0.0 all-gather.2.cloned.1.call-update
  10.2 7.5 %all-to-all-start = ((bf16[16,4,16,1024]{3,2,1,0:T(8,128)(2,1)}), bf16[16,4,16,1024]{3,2,1,0:T(8,128)(2,1)S(1)}, u32[]{:S(2)}, u32[]{:S(2)}) async-start(bf16[16,4,16,1024]{3,2,1,0:T(8,128)(2,1)} %get-tuple-element.14), calls=%async_computation | async-start | bytes 4194304 | tf_op jit(solution)/shard_map/all_to_all | solution.py:260
  17.6 0.5 collective-permute-start.1
  18.1 0.1 copy.16
  18.2 0.1 reshape.37
  18.3 1.9 collective-permute-start.2
  20.2 5.5 %collective-permute-done.2 = s32[1,8]{1,0:T(1,128)S(1)} collective-permute-done((s32[1,8]{1,0:T(1,128)S(1)}, s32[1,8]{1,0:T(1,128)S(1)}, u32[]{:S(2)}, u32[]{:S(2)}) %collective-permute-start.2) | collective-permute-done | bytes 64 | tf_op jit(solution)/shard_map/ppermute | solution.py:267
  25.7 0.1 collective-permute-start.3
  25.8 5.7 %collective-permute-done.3 = s32[2,8]{1,0:T(2,128)S(1)} collective-permute-done((s32[2,8]{1,0:T(2,128)S(1)}, s32[2,8]{1,0:T(2,128)S(1)}, u32[]{:S(2)}, u32[]{:S(2)}) %collective-permute-start.3) | collective-permute-done | bytes 96 | tf_op jit(solution)/shard_map/ppermute | solution.py:267
  31.5 4.7 %collective-permute-start.4 = (s32[4,8]{1,0:T(4,128)S(1)}, s32[4,8]{1,0:T(4,128)S(1)}, u32[]{:S(2)}, u32[]{:S(2)}) collective-permute-start(s32[4,8]{1,0:T(4,128)S(1)} %pad_add_fusion.1), channel_id=1, source_target_pairs={{0,8},{2,10},{4,12},{6,14},{8,0},{10,2},{12,4},{14,6},{1,9},{3,11}... | collective-permute-start | bytes 392 | tf_op jit(solution)/shard_map/ppermute | solution.py:267
  36.1 2.9 %collective-permute-done.4 = s32[4,8]{1,0:T(4,128)S(1)} collective-permute-done((s32[4,8]{1,0:T(4,128)S(1)}, s32[4,8]{1,0:T(4,128)S(1)}, u32[]{:S(2)}, u32[]{:S(2)}) %collective-permute-start.4) | collective-permute-done | bytes 160 | tf_op jit(solution)/shard_map/ppermute | solution.py:267
  39.1 0.1 copy.17
  39.2 0.1 copy.18
  39.3 0.1 reshape.39.where_ref
  39.4 8.7 %all-to-all-done = bf16[16,4,16,1024]{3,2,1,0:T(8,128)(2,1)S(1)} async-done(((bf16[16,4,16,1024]{3,2,1,0:T(8,128)(2,1)}), bf16[16,4,16,1024]{3,2,1,0:T(8,128)(2,1)S(1)}, u32[]{:S(2)}, u32[]{:S(2)}) %all-to-all-start) | async-done | bytes 2097184 | tf_op jit(solution)/shard_map/all_to_all | solution.py:260
  48.1 0.7 pick.1
  48.8 0.0 copy-start
  48.8 0.0 copy-start.1
  48.8 37.8 %all_to_all.30 = bf16[8,4,16,1024]{3,2,1,0:T(8,128)(2,1)} all-to-all(bf16[8,4,16,1024]{3,2,1,0:T(8,128)(2,1)S(1)} %get-tuple-element.15), channel_id=1, replica_groups=mesh['store'=16,'batch'=8,'space'=2] {'batch'}, dimensions={0} | all-to-all | bytes 2097152 | tf_op jit(solution)/shard_map/all_to_all | solution.py:287
  86.6 4.3 %all-to-all-start.2 = ((bf16[8,4,16,1024]{3,2,1,0:T(8,128)(2,1)}), bf16[8,4,16,1024]{3,2,1,0:T(8,128)(2,1)}, u32[]{:S(2)}, u32[]{:S(2)}) async-start(bf16[8,4,16,1024]{3,2,1,0:T(8,128)(2,1)} %copy-done.2), calls=%async_computation.2 | async-start | bytes 2097152 | tf_op jit(solution)/shard_map/all_to_all | solution.py:287
  90.8 0.3 collective-permute-start.5
  91.1 3.0 %collective-permute-done.5.refs_5_ = bf16[8,2,32,1024]{3,2,1,0:T(8,128)(2,1)} collective-permute-done((bf16[8,2,32,1024]{3,2,1,0:T(8,128)(2,1)}, bf16[8,2,32,1024]{3,2,1,0:T(8,128)(2,1)}, u32[]{:S(2)}, u32[]{:S(2)}) %collective-permute-start.5) | collective-permute-done | bytes 1048608 | tf_op jit(solution)/shard_map/ppermute | solution.py:292
  94.1 19.6 %attention.2 = (bf16[2,128,512]{2,1,0:T(8,128)(2,1)S(1)}, bf16[2,128,512]{2,1,0:T(8,128)(2,1)S(1)}, f32[3,1024,512]{2,1,0:T(8,128)}) custom-call(s32[1]{0:T(128)} %bitcast.core_ref, bf16[4,128,1024]{2,1,0:T(8,128)(2,1)S(1)} %copy-done, bf16[4,128,1024]{2,1,0:T(8,128)(2,1)S(1)} %collective-permute-done.refs_0_.refs_1_, bf16[4,128,1024]{2,1,0:T(8,128)(2,1)S(1)} %copy-done.1, ...), custom_call_target="tpu_custom_call" | custom-call | flops 5368709120 | bytes 16777216 | tf_op jit(solution)/shard_map/attention/pallas_call | solution.py:198
  113.7 0.7 copy-done.3
  114.4 0.7 copy-done.7
  115.1 3.3 %all-to-all-done.2 = bf16[8,4,16,1024]{3,2,1,0:T(8,128)(2,1)} async-done(((bf16[8,4,16,1024]{3,2,1,0:T(8,128)(2,1)}), bf16[8,4,16,1024]{3,2,1,0:T(8,128)(2,1)}, u32[]{:S(2)}, u32[]{:S(2)}) %all-to-all-start.2) | async-done | bytes 1048608 | tf_op jit(solution)/shard_map/all_to_all | solution.py:287
  118.4 0.0 collective-permute-start.7
  118.5 2.9 %collective-permute-done.7.refs_5_ = bf16[8,2,32,1024]{3,2,1,0:T(8,128)(2,1)S(1)} collective-permute-done((bf16[8,2,32,1024]{3,2,1,0:T(8,128)(2,1)}, bf16[8,2,32,1024]{3,2,1,0:T(8,128)(2,1)S(1)}, u32[]{:S(2)}, u32[]{:S(2)}) %collective-permute-start.7) | collective-permute-done | bytes 1048608 | tf_op jit(solution)/shard_map/ppermute | solution.py:292
  121.3 1.0 copy-done.9
  122.3 20.0 %attention.3 = (bf16[2,128,512]{2,1,0:T(8,128)(2,1)S(1)}, bf16[2,128,512]{2,1,0:T(8,128)(2,1)S(1)}, bf16[16,3,64,512]{3,2,1,0:T(8,128)(2,1)}) custom-call(s32[1]{0:T(128)} %bitcast.core_ref, bf16[4,128,1024]{2,1,0:T(8,128)(2,1)S(1)} %copy-done, bf16[4,128,1024]{2,1,0:T(8,128)(2,1)S(1)} %collective-permute-done.refs_0_.refs_1_, ...), custom_call_target="tpu_custom_call" | custom-call | flops 5368709120 | bytes 16777216 | tf_op jit(solution)/shard_map/attention/pallas_call | solution.py:198
  142.3 43.8 %all_to_all.31 = bf16[16,3,64,512]{3,2,1,0:T(8,128)(2,1)S(1)} all-to-all(bf16[16,3,64,512]{3,2,1,0:T(8,128)(2,1)} %get-tuple-element.23), channel_id=1, replica_groups=mesh['store'=16,'batch'=8,'space'=2] {'store'}, dimensions={0} | all-to-all | bytes 6291456 | tf_op jit(solution)/shard_map/all_to_all | solution.py:310
  186.1 0.5 convert_reduce_fusion
  186.7 0.8 copy_bitcast_fusion
  187.4 3.5 %all-to-all-start.4 = ((f32[8,3,8,512]{3,2,1,0:T(8,128)}), f32[8,3,8,512]{3,2,1,0:T(8,128)S(1)}, u32[]{:S(2)}, u32[]{:S(2)}) async-start(f32[8,3,8,512]{3,2,1,0:T(8,128)} %copy_bitcast_fusion), calls=%async_computation.4 | async-start | bytes 786432 | tf_op jit(solution)/shard_map/all_to_all | solution.py:314
  191.0 1.7 fusion.2
  192.7 0.1 collective-permute-start.6
  192.8 1.7 fusion.3
  194.5 0.6 collective-permute-start.8
  195.1 10.3 %all-to-all-done.4.parts_ref = f32[8,3,8,512]{3,2,1,0:T(8,128)S(1)} async-done(((f32[8,3,8,512]{3,2,1,0:T(8,128)}), f32[8,3,8,512]{3,2,1,0:T(8,128)S(1)}, u32[]{:S(2)}, u32[]{:S(2)}) %all-to-all-start.4) | async-done | bytes 393248 | tf_op jit(solution)/shard_map/all_to_all | solution.py:314
  205.4 0.8 total.1
  206.1 3.5 %all-to-all-start.5 = ((f32[8,3,8,512]{3,2,1,0:T(8,128)}), f32[8,3,8,512]{3,2,1,0:T(8,128)S(1)}, u32[]{:S(2)}, u32[]{:S(2)}) async-start(f32[8,3,8,512]{3,2,1,0:T(8,128)} %total.1), calls=%async_computation.5 | async-start | bytes 786432 | tf_op jit(solution)/shard_map/all_to_all | solution.py:315
  209.6 1.7 fusion.5
  211.3 1.7 fusion.4
  213.0 1.1 pad_maximum_fusion
  214.1 8.8 %all-to-all-done.5 = f32[8,3,8,512]{3,2,1,0:T(8,128)S(1)} async-done(((f32[8,3,8,512]{3,2,1,0:T(8,128)}), f32[8,3,8,512]{3,2,1,0:T(8,128)S(1)}, u32[]{:S(2)}, u32[]{:S(2)}) %all-to-all-start.5) | async-done | bytes 393248 | tf_op jit(solution)/shard_map/all_to_all | solution.py:315
  222.9 0.8 slice_bitcast_fusion.5
  (32 shorter events, 0.1 us)
Async XLA Ops:
  7.2 11.0 %copy-start.10 = (s32[4,2]{0,1:T(2,128)S(1)}, s32[4,2]{0,1:T(2,128)}, u32[]{:S(2)}) copy-start(s32[4,2]{0,1:T(2,128)} %param.11) | copy-start | bytes 100
  7.2 11.0 %copy-start.11 = (s32[4,2]{0,1:T(2,128)S(1)}, s32[4,2]{0,1:T(2,128)}, u32[]{:S(2)}) copy-start(s32[4,2]{0,1:T(2,128)} %param.10) | copy-start | bytes 100
  7.2 86.9 %all-gather.2.cloned.1.call-start = ((), (), s32[]{:S(2)}) async-start(), calls=%async_computation.6 | async-start | bytes 3342336 | tf_op jit(solution)/shard_map/all_gather | solution.py:281
  10.2 37.9 %all-to-all-start = ((bf16[16,4,16,1024]{3,2,1,0:T(8,128)(2,1)}), bf16[16,4,16,1024]{3,2,1,0:T(8,128)(2,1)S(1)}, u32[]{:S(2)}, u32[]{:S(2)}) async-start(bf16[16,4,16,1024]{3,2,1,0:T(8,128)(2,1)} %get-tuple-element.14), calls=%async_computation | async-start | bytes 4194304 | tf_op jit(solution)/shard_map/all_to_all | solution.py:260
  17.6 21.7 %collective-permute-start = (bf16[4,128,1024]{2,1,0:T(8,128)(2,1)}, bf16[4,128,1024]{2,1,0:T(8,128)(2,1)S(1)}, u32[]{:S(2)}, u32[]{:S(2)}) collective-permute-start(bf16[4,128,1024]{2,1,0:T(8,128)(2,1)} %refs_0_.3), channel_id=1, source_target_pairs={{0,1},{1,0},{2,3},{3,2},{4,5},{5,4},{6,7},{7,6},{8,9},{9,8},{10,11... | collective-permute-start | bytes 3145736 | tf_op jit(solution)/shard_map/ppermute | solution.py:277
  17.6 21.7 %collective-permute-start.1 = (bf16[4,128,1024]{2,1,0:T(8,128)(2,1)}, bf16[4,128,1024]{2,1,0:T(8,128)(2,1)}, u32[]{:S(2)}, u32[]{:S(2)}) collective-permute-start(bf16[4,128,1024]{2,1,0:T(8,128)(2,1)} %refs_2_.3), channel_id=1, source_target_pairs={{0,1},{1,0},{2,3},{3,2},{4,5},{5,4},{6,7},{7,6},{8,9},{9,8},{10,11... | collective-permute-start | bytes 3145736 | tf_op jit(solution)/shard_map/ppermute | solution.py:278
  18.3 7.4 %collective-permute-start.2 = (s32[1,8]{1,0:T(1,128)S(1)}, s32[1,8]{1,0:T(1,128)S(1)}, u32[]{:S(2)}, u32[]{:S(2)}) collective-permute-start(s32[1,8]{1,0:T(1,128)S(1)} %reshape.37), channel_id=1, source_target_pairs={{0,2},{2,4},{4,6},{6,8},{8,10},{10,12},{12,14},{14,0},{1,3},{3,5},... | collective-permute-start | bytes 104 | tf_op jit(solution)/shard_map/ppermute | solution.py:267
  25.7 5.8 %collective-permute-start.3 = (s32[2,8]{1,0:T(2,128)S(1)}, s32[2,8]{1,0:T(2,128)S(1)}, u32[]{:S(2)}, u32[]{:S(2)}) collective-permute-start(s32[2,8]{1,0:T(2,128)S(1)} %pad_add_fusion.2), channel_id=1, source_target_pairs={{0,4},{2,6},{4,8},{6,10},{8,12},{10,14},{12,0},{14,2},{1,5},{3,7},... | collective-permute-start | bytes 200 | tf_op jit(solution)/shard_map/ppermute | solution.py:267
  31.5 7.6 %collective-permute-start.4 = (s32[4,8]{1,0:T(4,128)S(1)}, s32[4,8]{1,0:T(4,128)S(1)}, u32[]{:S(2)}, u32[]{:S(2)}) collective-permute-start(s32[4,8]{1,0:T(4,128)S(1)} %pad_add_fusion.1), channel_id=1, source_target_pairs={{0,8},{2,10},{4,12},{6,14},{8,0},{10,2},{12,4},{14,6},{1,9},{3,11}... | collective-permute-start | bytes 392 | tf_op jit(solution)/shard_map/ppermute | solution.py:267
  48.7 37.8 %copy-start.2 = (bf16[8,4,16,1024]{3,2,1,0:T(8,128)(2,1)}, bf16[8,4,16,1024]{3,2,1,0:T(8,128)(2,1)S(1)}, u32[]{:S(2)}) copy-start(bf16[8,4,16,1024]{3,2,1,0:T(8,128)(2,1)S(1)} %get-tuple-element.19) | copy-start | bytes 3145732
  48.8 45.4 %copy-start = (bf16[4,128,1024]{2,1,0:T(8,128)(2,1)S(1)}, bf16[4,128,1024]{2,1,0:T(8,128)(2,1)}, u32[]{:S(2)}) copy-start(bf16[4,128,1024]{2,1,0:T(8,128)(2,1)} %refs_0_.3) | copy-start | bytes 3145732
  48.8 45.3 %copy-start.1 = (bf16[4,128,1024]{2,1,0:T(8,128)(2,1)S(1)}, bf16[4,128,1024]{2,1,0:T(8,128)(2,1)}, u32[]{:S(2)}) copy-start(bf16[4,128,1024]{2,1,0:T(8,128)(2,1)} %refs_2_.3) | copy-start | bytes 3145732
  86.6 31.9 %all-to-all-start.2 = ((bf16[8,4,16,1024]{3,2,1,0:T(8,128)(2,1)}), bf16[8,4,16,1024]{3,2,1,0:T(8,128)(2,1)}, u32[]{:S(2)}, u32[]{:S(2)}) async-start(bf16[8,4,16,1024]{3,2,1,0:T(8,128)(2,1)} %copy-done.2), calls=%async_computation.2 | async-start | bytes 2097152 | tf_op jit(solution)/shard_map/all_to_all | solution.py:287
  90.8 3.3 %collective-permute-start.5 = (bf16[8,2,32,1024]{3,2,1,0:T(8,128)(2,1)}, bf16[8,2,32,1024]{3,2,1,0:T(8,128)(2,1)}, u32[]{:S(2)}, u32[]{:S(2)}) collective-permute-start(bf16[8,2,32,1024]{3,2,1,0:T(8,128)(2,1)} %bitcast.30), channel_id=1, source_target_pairs={{0,1},{1,0},{2,3},{3,2},{4,5},{5,4},{6,7},{7,6},{8,9},{9,8},{10,11... | collective-permute-start | bytes 3145736 | tf_op jit(solution)/shard_map/ppermute | solution.py:292
  113.7 0.7 copy-start.3
  114.4 0.7 copy-start.7
  118.4 2.9 %collective-permute-start.7 = (bf16[8,2,32,1024]{3,2,1,0:T(8,128)(2,1)}, bf16[8,2,32,1024]{3,2,1,0:T(8,128)(2,1)S(1)}, u32[]{:S(2)}, u32[]{:S(2)}) collective-permute-start(bf16[8,2,32,1024]{3,2,1,0:T(8,128)(2,1)} %hold.1.refs_4_), channel_id=1, source_target_pairs={{0,1},{1,0},{2,3},{3,2},{4,5},{5,4},{6,7},{7,6},{8,9},{9,8},{10,11... | collective-permute-start | bytes 3145736 | tf_op jit(solution)/shard_map/ppermute | solution.py:292
  121.3 1.0 copy-start.9
  142.3 43.8 %copy-start.5 = (bf16[2,128,512]{2,1,0:T(8,128)(2,1)}, bf16[2,128,512]{2,1,0:T(8,128)(2,1)S(1)}, u32[]{:S(2)}) copy-start(bf16[2,128,512]{2,1,0:T(8,128)(2,1)S(1)} %get-tuple-element.22) | copy-start | bytes 786436
  186.1 4.8 %copy-start.8 = (bf16[2,128,512]{2,1,0:T(8,128)(2,1)S(1)}, bf16[2,128,512]{2,1,0:T(8,128)(2,1)}, u32[]{:S(2)}) copy-start(bf16[2,128,512]{2,1,0:T(8,128)(2,1)} %copy-done.7) | copy-start | bytes 786436
  186.6 6.2 %copy-start.6 = (bf16[2,128,512]{2,1,0:T(8,128)(2,1)S(1)}, bf16[2,128,512]{2,1,0:T(8,128)(2,1)}, u32[]{:S(2)}) copy-start(bf16[2,128,512]{2,1,0:T(8,128)(2,1)} %copy-done.5) | copy-start | bytes 786436
  187.4 17.9 %all-to-all-start.4 = ((f32[8,3,8,512]{3,2,1,0:T(8,128)}), f32[8,3,8,512]{3,2,1,0:T(8,128)S(1)}, u32[]{:S(2)}, u32[]{:S(2)}) async-start(f32[8,3,8,512]{3,2,1,0:T(8,128)} %copy_bitcast_fusion), calls=%async_computation.4 | async-start | bytes 786432 | tf_op jit(solution)/shard_map/all_to_all | solution.py:314
  191.0 18.7 %copy-start.4 = (bf16[2,128,512]{2,1,0:T(8,128)(2,1)S(1)}, bf16[2,128,512]{2,1,0:T(8,128)(2,1)}, u32[]{:S(2)}) copy-start(bf16[2,128,512]{2,1,0:T(8,128)(2,1)} %copy-done.3) | copy-start | bytes 786436
  192.7 16.9 %collective-permute-start.6 = (bf16[2,128,1024]{2,1,0:T(8,128)(2,1)S(1)}, bf16[2,128,1024]{2,1,0:T(8,128)(2,1)S(1)}, u32[]{:S(2)}, u32[]{:S(2)}) collective-permute-start(bf16[2,128,1024]{2,1,0:T(8,128)(2,1)S(1)} %fusion.2), channel_id=1, source_target_pairs={{0,1},{1,0},{2,3},{3,2},{4,5},{5,4},{6,7},{7,6},{8,9},{9,8},{10,11... | collective-permute-start | bytes 1572872 | tf_op jit(solution)/shard_map/ppermute | solution.py:305
  194.5 16.8 %collective-permute-start.8 = (bf16[2,128,1024]{2,1,0:T(8,128)(2,1)S(1)}, bf16[2,128,1024]{2,1,0:T(8,128)(2,1)S(1)}, u32[]{:S(2)}, u32[]{:S(2)}) collective-permute-start(bf16[2,128,1024]{2,1,0:T(8,128)(2,1)S(1)} %fusion.3), channel_id=1, source_target_pairs={{0,1},{1,0},{2,3},{3,2},{4,5},{5,4},{6,7},{7,6},{8,9},{9,8},{10,11... | collective-permute-start | bytes 1572872 | tf_op jit(solution)/shard_map/ppermute | solution.py:305
  206.1 16.8 %all-to-all-start.5 = ((f32[8,3,8,512]{3,2,1,0:T(8,128)}), f32[8,3,8,512]{3,2,1,0:T(8,128)S(1)}, u32[]{:S(2)}, u32[]{:S(2)}) async-start(f32[8,3,8,512]{3,2,1,0:T(8,128)} %total.1), calls=%async_computation.5 | async-start | bytes 786432 | tf_op jit(solution)/shard_map/all_to_all | solution.py:315
Sparse Core Ops, SparseCore 0:
  10.4 67.0 all-gather.1

commit v4 on v3

--- a/solution.py
+++ b/solution.py
@@ -109,48 +109,57 @@
         v_s[i] = v.reshape(layers, prompts, rows, width)
     scale = HD ** (-0.5)
     lane = lax.broadcasted_iota(jnp.int32, (1, 2 * HD), 1)
-    first = lane < HD
+    keeps = [jnp.where(lane < HD, 1.0, 0.0), jnp.where(lane < HD, 0.0, 1.0)]
 
     def both(array):
         return jnp.concatenate([array[0], array[1]], axis=0)
 
-    for p in range(prompts):
-        for pair in range(width // (2 * HD)):
-            cols = pl.ds(pair * 2 * HD, 2 * HD)
-            kp = both([k_s[i, :, p, :, cols].reshape(part, 2 * HD) for i in range(2)])
-            vp = both([v_s[i, :, p, :, cols].reshape(part, 2 * HD) for i in range(2)])
-            qp = both([q_s[i, p, :, cols] for i in range(2)])
-            up = both([uo[p, :, cols], ut[p, :, cols]])
-            kt = kp.T
-            grad_k = grad_v = None
-            grad_q = []
-            for side in range(2):
-                keep = jnp.where(first if side == 0 else jnp.logical_not(first), 1.0, 0.0)
-                qm = qp * (keep * scale).astype(BF16)
-                um = up * keep.astype(BF16)
-                s = lax.dot_general(kp, qm, NT, preferred_element_type=F32)
-                dw = lax.dot_general(vp, um, NT, preferred_element_type=F32)
-                e = jnp.exp(s - jnp.max(s, axis=0, keepdims=True))
-                inverse = 1.0 / jnp.sum(e, axis=0, keepdims=True)
-                att = e * inverse
-                row = jnp.sum(e * dw, axis=0, keepdims=True) * inverse
-                gv_part = jnp.dot(att.astype(BF16), um, preferred_element_type=F32)
-                ds = (att * (dw - row)).astype(BF16)
-                gk_part = jnp.dot(ds, qm, preferred_element_type=F32)
-                grad_q.append(
-                    jnp.dot(kt[side * HD : (side + 1) * HD], ds, preferred_element_type=F32)
-                )
-                grad_v = gv_part if grad_v is None else grad_v + gv_part
-                grad_k = gk_part if grad_k is None else grad_k + gk_part
-            gq = (both(grad_q) * scale).T.astype(BF16)
-            gk, gv = grad_k.astype(BF16), grad_v.astype(BF16)
-            more = pl.ds(width + pair * 2 * HD, 2 * HD)
-            for i, out in enumerate((gqo, gqt)):
-                out[p, :, cols] = gq[i * half : (i + 1) * half]
-                gq_s[i, p, :, cols] = gq[i * half : (i + 1) * half]
-                here = slice(i * part, (i + 1) * part)
-                gkv_s[i, :, p, :, cols] = gk[here].reshape(layers, rows, 2 * HD)
-                gkv_s[i, :, p, :, more] = gv[here].reshape(layers, rows, 2 * HD)
+    def start(p, pair):
+        cols = pl.ds(pair * 2 * HD, 2 * HD)
+        kp = both([k_s[i, :, p, :, cols].reshape(part, 2 * HD) for i in range(2)])
+        vp = both([v_s[i, :, p, :, cols].reshape(part, 2 * HD) for i in range(2)])
+        qp = both([q_s[i, p, :, cols] for i in range(2)])
+        up = both([uo[p, :, cols], ut[p, :, cols]])
+        qm = [qp * (k * scale).astype(BF16) for k in keeps]
+        um = [up * k.astype(BF16) for k in keeps]
+        s = [lax.dot_general(kp, q, NT, preferred_element_type=F32) for q in qm]
+        dw = [lax.dot_general(vp, u, NT, preferred_element_type=F32) for u in um]
+        return kp, qm, um, s, dw
+
+    def finish(p, pair, kp, qm, um, s, dw):
+        cols = pl.ds(pair * 2 * HD, 2 * HD)
+        kt = kp.T
+        grad_k = grad_v = None
+        grad_q = []
+        for side in range(2):
+            e = jnp.exp(s[side] - jnp.max(s[side], axis=0, keepdims=True))
+            inverse = 1.0 / jnp.sum(e, axis=0, keepdims=True)
+            att = e * inverse
+            row = jnp.sum(e * dw[side], axis=0, keepdims=True) * inverse
+            gv_part = jnp.dot(att.astype(BF16), um[side], preferred_element_type=F32)
+            ds = (att * (dw[side] - row)).astype(BF16)
+            gk_part = jnp.dot(ds, qm[side], preferred_element_type=F32)
+            grad_q.append(
+                jnp.dot(kt[side * HD : (side + 1) * HD], ds, preferred_element_type=F32)
+            )
+            grad_v = gv_part if grad_v is None else grad_v + gv_part
+            grad_k = gk_part if grad_k is None else grad_k + gk_part
+        gq = (both(grad_q) * scale).T.astype(BF16)
+        gk, gv = grad_k.astype(BF16), grad_v.astype(BF16)
+        more = pl.ds(width + pair * 2 * HD, 2 * HD)
+        for i, out in enumerate((gqo, gqt)):
+            out[p, :, cols] = gq[i * half : (i + 1) * half]
+            gq_s[i, p, :, cols] = gq[i * half : (i + 1) * half]
+            here = slice(i * part, (i + 1) * part)
+            gkv_s[i, :, p, :, cols] = gk[here].reshape(layers, rows, 2 * HD)
+            gkv_s[i, :, p, :, more] = gv[here].reshape(layers, rows, 2 * HD)
+
+    units = [(p, pair) for p in range(prompts) for pair in range(width // (2 * HD))]
+    held = start(*units[0])
+    for i, unit in enumerate(units):
+        later = start(*units[i + 1]) if i + 1 < len(units) else None
+        finish(*unit, *held)
+        held = later
     gq_all = gq_s[...].reshape(2 * prompts * half, width)
     gkv_all = gkv_s[...].reshape(2 * prompts * part, 2 * width)
     block = 256

time: 231 us -> 229 us (level)
  Pallas kernels: 44 us -> 38.8 us
  waiting for transfers between devices: 51 us -> 53.8 us
    pallas_call x2, Pallas kernels: 39.6 us -> 34.5 us  [attention(): pl.pallas_call(functools.partial(attention_kernel, has_before), out_shape...]
    all_to_all x1, waiting for transfers between devices: 3.33 us -> 5.93 us  [per_device(): lax.all_to_all(picked[chunk], 'batch', split_axis=0, concat_axis=0, tiled...]
  transfers between devices with their start and end apart: 14 -> 14, of which waited for: 9 -> 9; matrix products, arithmetic and copies ran while one was open for 4% -> 4% of each run, Pallas kernels for 9% -> 8%
where the time goes in v4:
time: 229 us; the launch traced here: 228 us
  blocking collectives  81.6 us (36%)
  waiting for transfers between devices  53.8 us (23%)
  Pallas kernels  38.8 us (17%)
  starting transfers between devices  26.6 us (12%)
  between operations  14.3 us (6%)
  matrix products  6.81 us (3%)
  local copies, waits for them, and re-layouts  4.39 us (2%)
    all_to_all x1, blocking collectives, per_device(): lax.all_to_all(sums, 'store', split_axis=0, concat_axis=0, tiled=True)  43.8 us
    all_to_all x1, blocking collectives, per_device(): lax.all_to_all(picked[chunk], 'batch', split_axis=0, concat_axis=0, tiled...  37.8 us
    pallas_call x2, Pallas kernels, attention(): pl.pallas_call(functools.partial(attention_kernel, has_before), out_shape...  34.5 us
    ppermute x3, waiting for transfers between devices, per_device(): lax.ppermute(listed, 'batch', [(z, (z + reach) % layers) for z in range(l...  14 us
    all_to_all x1, waiting for transfers between devices, per_device(): lax.all_to_all(pieces, 'batch', split_axis=0, concat_axis=0, tiled=True)  10.3 us
    all_to_all x1, waiting for transfers between devices, per_device(): lax.all_to_all(total_for_all(crossed), 'batch', split_axis=0, concat_axis...  9.02 us
    all_to_all x1, waiting for transfers between devices, per_device(): lax.all_to_all(spread, 'store', split_axis=0, concat_axis=0, tiled=True)  8.68 us
    all_to_all x1, starting transfers between devices, per_device(): lax.all_to_all(spread, 'store', split_axis=0, concat_axis=0, tiled=True)  7.46 us
  transfers between devices with their start and end apart: 14, of which 9 were waited for; matrix products, arithmetic and copies ran while one was open for 4% of the time, Pallas kernels for 8%

profile of v4, /device:TPU:4, one launch (start us, length us, event | category | flops | bytes accessed | tf_op | source)
XLA Modules:
  0.0 227.9 jit_solution(6837845426276563570)
XLA Ops:
  7.2 0.0 all-gather.2.cloned.1.call-start
  7.2 2.9 %prepare.1 = (bf16[16,4,16,1024]{3,2,1,0:T(8,128)(2,1)}, bf16[64,1536]{1,0:T(8,128)(2,1)}) custom-call(s32[1]{0:T(128)} %bitcast.3.layer_ref, bf16[4,128,1024]{2,1,0:T(8,128)(2,1)} %maps_ref.1, bf16[64,512]{1,0:T(8,128)(2,1)} %wq.1, bf16[64,512]{1,0:T(8,128)(2,1)} %wk.1, bf16[64,512]{1,0:T(8,128)(2,1)} %wv.1), custom_call_target="tpu_custom_call" | custom-call | tf_op jit(solution)/shard_map/prepare/pallas_call | solution.py:37
  10.1 0.0 all-gather.2.cloned.1.call-update
  10.2 7.5 %all-to-all-start = ((bf16[16,4,16,1024]{3,2,1,0:T(8,128)(2,1)}), bf16[16,4,16,1024]{3,2,1,0:T(8,128)(2,1)S(1)}, u32[]{:S(2)}, u32[]{:S(2)}) async-start(bf16[16,4,16,1024]{3,2,1,0:T(8,128)(2,1)} %get-tuple-element.14), calls=%async_computation | async-start | bytes 4194304 | tf_op jit(solution)/shard_map/all_to_all | solution.py:269
  17.6 0.5 collective-permute-start.1
  18.1 0.1 copy.16
  18.2 0.1 reshape.37
  18.3 1.9 collective-permute-start.2
  20.2 5.5 %collective-permute-done.2 = s32[1,8]{1,0:T(1,128)S(1)} collective-permute-done((s32[1,8]{1,0:T(1,128)S(1)}, s32[1,8]{1,0:T(1,128)S(1)}, u32[]{:S(2)}, u32[]{:S(2)}) %collective-permute-start.2) | collective-permute-done | bytes 64 | tf_op jit(solution)/shard_map/ppermute | solution.py:276
  25.7 0.1 collective-permute-start.3
  25.8 5.7 %collective-permute-done.3 = s32[2,8]{1,0:T(2,128)S(1)} collective-permute-done((s32[2,8]{1,0:T(2,128)S(1)}, s32[2,8]{1,0:T(2,128)S(1)}, u32[]{:S(2)}, u32[]{:S(2)}) %collective-permute-start.3) | collective-permute-done | bytes 96 | tf_op jit(solution)/shard_map/ppermute | solution.py:276
  31.5 4.7 %collective-permute-start.4 = (s32[4,8]{1,0:T(4,128)S(1)}, s32[4,8]{1,0:T(4,128)S(1)}, u32[]{:S(2)}, u32[]{:S(2)}) collective-permute-start(s32[4,8]{1,0:T(4,128)S(1)} %pad_add_fusion.1), channel_id=1, source_target_pairs={{0,8},{2,10},{4,12},{6,14},{8,0},{10,2},{12,4},{14,6},{1,9},{3,11}... | collective-permute-start | bytes 392 | tf_op jit(solution)/shard_map/ppermute | solution.py:276
  36.1 2.9 %collective-permute-done.4 = s32[4,8]{1,0:T(4,128)S(1)} collective-permute-done((s32[4,8]{1,0:T(4,128)S(1)}, s32[4,8]{1,0:T(4,128)S(1)}, u32[]{:S(2)}, u32[]{:S(2)}) %collective-permute-start.4) | collective-permute-done | bytes 160 | tf_op jit(solution)/shard_map/ppermute | solution.py:276
  39.1 0.1 copy.17
  39.2 0.1 copy.18
  39.3 0.1 reshape.39.where_ref
  39.4 8.7 %all-to-all-done = bf16[16,4,16,1024]{3,2,1,0:T(8,128)(2,1)S(1)} async-done(((bf16[16,4,16,1024]{3,2,1,0:T(8,128)(2,1)}), bf16[16,4,16,1024]{3,2,1,0:T(8,128)(2,1)S(1)}, u32[]{:S(2)}, u32[]{:S(2)}) %all-to-all-start) | async-done | bytes 2097184 | tf_op jit(solution)/shard_map/all_to_all | solution.py:269
  48.1 0.7 pick.1
  48.8 0.0 copy-start
  48.8 0.0 copy-start.1
  48.8 37.8 %all_to_all.30 = bf16[8,4,16,1024]{3,2,1,0:T(8,128)(2,1)} all-to-all(bf16[8,4,16,1024]{3,2,1,0:T(8,128)(2,1)S(1)} %get-tuple-element.15), channel_id=1, replica_groups=mesh['store'=16,'batch'=8,'space'=2] {'batch'}, dimensions={0} | all-to-all | bytes 2097152 | tf_op jit(solution)/shard_map/all_to_all | solution.py:296
  86.6 4.3 %all-to-all-start.2 = ((bf16[8,4,16,1024]{3,2,1,0:T(8,128)(2,1)}), bf16[8,4,16,1024]{3,2,1,0:T(8,128)(2,1)}, u32[]{:S(2)}, u32[]{:S(2)}) async-start(bf16[8,4,16,1024]{3,2,1,0:T(8,128)(2,1)} %copy-done.2), calls=%async_computation.2 | async-start | bytes 2097152 | tf_op jit(solution)/shard_map/all_to_all | solution.py:296
  90.8 0.1 collective-permute-start.5
  90.9 3.0 %collective-permute-done.5.refs_5_ = bf16[8,2,32,1024]{3,2,1,0:T(8,128)(2,1)} collective-permute-done((bf16[8,2,32,1024]{3,2,1,0:T(8,128)(2,1)}, bf16[8,2,32,1024]{3,2,1,0:T(8,128)(2,1)}, u32[]{:S(2)}, u32[]{:S(2)}) %collective-permute-start.5) | collective-permute-done | bytes 1048608 | tf_op jit(solution)/shard_map/ppermute | solution.py:301
  93.9 17.1 %attention.2 = (bf16[2,128,512]{2,1,0:T(8,128)(2,1)S(1)}, bf16[2,128,512]{2,1,0:T(8,128)(2,1)S(1)}, f32[3,1024,512]{2,1,0:T(8,128)}) custom-call(s32[1]{0:T(128)} %bitcast.core_ref, bf16[4,128,1024]{2,1,0:T(8,128)(2,1)S(1)} %copy-done, bf16[4,128,1024]{2,1,0:T(8,128)(2,1)S(1)} %collective-permute-done.refs_0_.refs_1_, bf16[4,128,1024]{2,1,0:T(8,128)(2,1)S(1)} %copy-done.1, ...), custom_call_target="tpu_custom_call" | custom-call | flops 5368709120 | bytes 16777216 | tf_op jit(solution)/shard_map/attention/pallas_call | solution.py:207
  111.1 0.7 copy-done.3
  111.8 0.7 copy-done.7
  112.5 5.9 %all-to-all-done.2 = bf16[8,4,16,1024]{3,2,1,0:T(8,128)(2,1)} async-done(((bf16[8,4,16,1024]{3,2,1,0:T(8,128)(2,1)}), bf16[8,4,16,1024]{3,2,1,0:T(8,128)(2,1)}, u32[]{:S(2)}, u32[]{:S(2)}) %all-to-all-start.2) | async-done | bytes 1048608 | tf_op jit(solution)/shard_map/all_to_all | solution.py:296
  118.4 0.0 collective-permute-start.7
  118.5 2.9 %collective-permute-done.7.refs_5_ = bf16[8,2,32,1024]{3,2,1,0:T(8,128)(2,1)S(1)} collective-permute-done((bf16[8,2,32,1024]{3,2,1,0:T(8,128)(2,1)}, bf16[8,2,32,1024]{3,2,1,0:T(8,128)(2,1)S(1)}, u32[]{:S(2)}, u32[]{:S(2)}) %collective-permute-start.7) | collective-permute-done | bytes 1048608 | tf_op jit(solution)/shard_map/ppermute | solution.py:301
  121.3 1.0 copy-done.9
  122.3 17.3 %attention.3 = (bf16[2,128,512]{2,1,0:T(8,128)(2,1)S(1)}, bf16[2,128,512]{2,1,0:T(8,128)(2,1)S(1)}, bf16[16,3,64,512]{3,2,1,0:T(8,128)(2,1)}) custom-call(s32[1]{0:T(128)} %bitcast.core_ref, bf16[4,128,1024]{2,1,0:T(8,128)(2,1)S(1)} %copy-done, bf16[4,128,1024]{2,1,0:T(8,128)(2,1)S(1)} %collective-permute-done.refs_0_.refs_1_, ...), custom_call_target="tpu_custom_call" | custom-call | flops 5368709120 | bytes 16777216 | tf_op jit(solution)/shard_map/attention/pallas_call | solution.py:207
  139.6 43.8 %all_to_all.31 = bf16[16,3,64,512]{3,2,1,0:T(8,128)(2,1)S(1)} all-to-all(bf16[16,3,64,512]{3,2,1,0:T(8,128)(2,1)} %get-tuple-element.23), channel_id=1, replica_groups=mesh['store'=16,'batch'=8,'space'=2] {'store'}, dimensions={0} | all-to-all | bytes 6291456 | tf_op jit(solution)/shard_map/all_to_all | solution.py:319
  183.4 0.5 convert_reduce_fusion
  183.9 0.8 copy_bitcast_fusion
  184.7 3.5 %all-to-all-start.4 = ((f32[8,3,8,512]{3,2,1,0:T(8,128)}), f32[8,3,8,512]{3,2,1,0:T(8,128)S(1)}, u32[]{:S(2)}, u32[]{:S(2)}) async-start(f32[8,3,8,512]{3,2,1,0:T(8,128)} %copy_bitcast_fusion), calls=%async_computation.4 | async-start | bytes 786432 | tf_op jit(solution)/shard_map/all_to_all | solution.py:323
  188.2 1.7 fusion.2
  189.9 0.1 collective-permute-start.6
  190.0 1.7 fusion.3
  191.7 0.6 collective-permute-start.8
  192.3 10.3 %all-to-all-done.4.parts_ref = f32[8,3,8,512]{3,2,1,0:T(8,128)S(1)} async-done(((f32[8,3,8,512]{3,2,1,0:T(8,128)}), f32[8,3,8,512]{3,2,1,0:T(8,128)S(1)}, u32[]{:S(2)}, u32[]{:S(2)}) %all-to-all-start.4) | async-done | bytes 393248 | tf_op jit(solution)/shard_map/all_to_all | solution.py:323
  202.6 0.8 total.1
  203.4 3.5 %all-to-all-start.5 = ((f32[8,3,8,512]{3,2,1,0:T(8,128)}), f32[8,3,8,512]{3,2,1,0:T(8,128)S(1)}, u32[]{:S(2)}, u32[]{:S(2)}) async-start(f32[8,3,8,512]{3,2,1,0:T(8,128)} %total.1), calls=%async_computation.5 | async-start | bytes 786432 | tf_op jit(solution)/shard_map/all_to_all | solution.py:324
  206.8 1.7 fusion.5
  208.6 1.7 fusion.4
  210.3 1.1 pad_maximum_fusion
  211.3 9.0 %all-to-all-done.5 = f32[8,3,8,512]{3,2,1,0:T(8,128)S(1)} async-done(((f32[8,3,8,512]{3,2,1,0:T(8,128)}), f32[8,3,8,512]{3,2,1,0:T(8,128)S(1)}, u32[]{:S(2)}, u32[]{:S(2)}) %all-to-all-start.5) | async-done | bytes 393248 | tf_op jit(solution)/shard_map/all_to_all | solution.py:324
  220.3 0.8 slice_bitcast_fusion.5
  (32 shorter events, 0.1 us)
Async XLA Ops:
  7.2 11.0 %copy-start.10 = (s32[4,2]{0,1:T(2,128)S(1)}, s32[4,2]{0,1:T(2,128)}, u32[]{:S(2)}) copy-start(s32[4,2]{0,1:T(2,128)} %param.11) | copy-start | bytes 100
  7.2 11.0 %copy-start.11 = (s32[4,2]{0,1:T(2,128)S(1)}, s32[4,2]{0,1:T(2,128)}, u32[]{:S(2)}) copy-start(s32[4,2]{0,1:T(2,128)} %param.10) | copy-start | bytes 100
  7.2 86.7 %all-gather.2.cloned.1.call-start = ((), (), s32[]{:S(2)}) async-start(), calls=%async_computation.6 | async-start | bytes 3342336 | tf_op jit(solution)/shard_map/all_gather | solution.py:290
  10.2 37.9 %all-to-all-start = ((bf16[16,4,16,1024]{3,2,1,0:T(8,128)(2,1)}), bf16[16,4,16,1024]{3,2,1,0:T(8,128)(2,1)S(1)}, u32[]{:S(2)}, u32[]{:S(2)}) async-start(bf16[16,4,16,1024]{3,2,1,0:T(8,128)(2,1)} %get-tuple-element.14), calls=%async_computation | async-start | bytes 4194304 | tf_op jit(solution)/shard_map/all_to_all | solution.py:269
  17.6 21.7 %collective-permute-start = (bf16[4,128,1024]{2,1,0:T(8,128)(2,1)}, bf16[4,128,1024]{2,1,0:T(8,128)(2,1)S(1)}, u32[]{:S(2)}, u32[]{:S(2)}) collective-permute-start(bf16[4,128,1024]{2,1,0:T(8,128)(2,1)} %refs_0_.3), channel_id=1, source_target_pairs={{0,1},{1,0},{2,3},{3,2},{4,5},{5,4},{6,7},{7,6},{8,9},{9,8},{10,11... | collective-permute-start | bytes 3145736 | tf_op jit(solution)/shard_map/ppermute | solution.py:286
  17.6 21.7 %collective-permute-start.1 = (bf16[4,128,1024]{2,1,0:T(8,128)(2,1)}, bf16[4,128,1024]{2,1,0:T(8,128)(2,1)}, u32[]{:S(2)}, u32[]{:S(2)}) collective-permute-start(bf16[4,128,1024]{2,1,0:T(8,128)(2,1)} %refs_2_.3), channel_id=1, source_target_pairs={{0,1},{1,0},{2,3},{3,2},{4,5},{5,4},{6,7},{7,6},{8,9},{9,8},{10,11... | collective-permute-start | bytes 3145736 | tf_op jit(solution)/shard_map/ppermute | solution.py:287
  18.3 7.4 %collective-permute-start.2 = (s32[1,8]{1,0:T(1,128)S(1)}, s32[1,8]{1,0:T(1,128)S(1)}, u32[]{:S(2)}, u32[]{:S(2)}) collective-permute-start(s32[1,8]{1,0:T(1,128)S(1)} %reshape.37), channel_id=1, source_target_pairs={{0,2},{2,4},{4,6},{6,8},{8,10},{10,12},{12,14},{14,0},{1,3},{3,5},... | collective-permute-start | bytes 104 | tf_op jit(solution)/shard_map/ppermute | solution.py:276
  25.7 5.8 %collective-permute-start.3 = (s32[2,8]{1,0:T(2,128)S(1)}, s32[2,8]{1,0:T(2,128)S(1)}, u32[]{:S(2)}, u32[]{:S(2)}) collective-permute-start(s32[2,8]{1,0:T(2,128)S(1)} %pad_add_fusion.2), channel_id=1, source_target_pairs={{0,4},{2,6},{4,8},{6,10},{8,12},{10,14},{12,0},{14,2},{1,5},{3,7},... | collective-permute-start | bytes 200 | tf_op jit(solution)/shard_map/ppermute | solution.py:276
  31.5 7.6 %collective-permute-start.4 = (s32[4,8]{1,0:T(4,128)S(1)}, s32[4,8]{1,0:T(4,128)S(1)}, u32[]{:S(2)}, u32[]{:S(2)}) collective-permute-start(s32[4,8]{1,0:T(4,128)S(1)} %pad_add_fusion.1), channel_id=1, source_target_pairs={{0,8},{2,10},{4,12},{6,14},{8,0},{10,2},{12,4},{14,6},{1,9},{3,11}... | collective-permute-start | bytes 392 | tf_op jit(solution)/shard_map/ppermute | solution.py:276
  48.7 37.8 %copy-start.2 = (bf16[8,4,16,1024]{3,2,1,0:T(8,128)(2,1)}, bf16[8,4,16,1024]{3,2,1,0:T(8,128)(2,1)S(1)}, u32[]{:S(2)}) copy-start(bf16[8,4,16,1024]{3,2,1,0:T(8,128)(2,1)S(1)} %get-tuple-element.19) | copy-start | bytes 3145732
  48.8 45.2 %copy-start = (bf16[4,128,1024]{2,1,0:T(8,128)(2,1)S(1)}, bf16[4,128,1024]{2,1,0:T(8,128)(2,1)}, u32[]{:S(2)}) copy-start(bf16[4,128,1024]{2,1,0:T(8,128)(2,1)} %refs_0_.3) | copy-start | bytes 3145732
  48.8 45.2 %copy-start.1 = (bf16[4,128,1024]{2,1,0:T(8,128)(2,1)S(1)}, bf16[4,128,1024]{2,1,0:T(8,128)(2,1)}, u32[]{:S(2)}) copy-start(bf16[4,128,1024]{2,1,0:T(8,128)(2,1)} %refs_2_.3) | copy-start | bytes 3145732
  86.6 31.9 %all-to-all-start.2 = ((bf16[8,4,16,1024]{3,2,1,0:T(8,128)(2,1)}), bf16[8,4,16,1024]{3,2,1,0:T(8,128)(2,1)}, u32[]{:S(2)}, u32[]{:S(2)}) async-start(bf16[8,4,16,1024]{3,2,1,0:T(8,128)(2,1)} %copy-done.2), calls=%async_computation.2 | async-start | bytes 2097152 | tf_op jit(solution)/shard_map/all_to_all | solution.py:296
  90.8 3.1 %collective-permute-start.5 = (bf16[8,2,32,1024]{3,2,1,0:T(8,128)(2,1)}, bf16[8,2,32,1024]{3,2,1,0:T(8,128)(2,1)}, u32[]{:S(2)}, u32[]{:S(2)}) collective-permute-start(bf16[8,2,32,1024]{3,2,1,0:T(8,128)(2,1)} %bitcast.30), channel_id=1, source_target_pairs={{0,1},{1,0},{2,3},{3,2},{4,5},{5,4},{6,7},{7,6},{8,9},{9,8},{10,11... | collective-permute-start | bytes 3145736 | tf_op jit(solution)/shard_map/ppermute | solution.py:301
  111.1 0.7 copy-start.3
  111.8 0.7 copy-start.7
  118.4 2.9 %collective-permute-start.7 = (bf16[8,2,32,1024]{3,2,1,0:T(8,128)(2,1)}, bf16[8,2,32,1024]{3,2,1,0:T(8,128)(2,1)S(1)}, u32[]{:S(2)}, u32[]{:S(2)}) collective-permute-start(bf16[8,2,32,1024]{3,2,1,0:T(8,128)(2,1)} %hold.1.refs_4_), channel_id=1, source_target_pairs={{0,1},{1,0},{2,3},{3,2},{4,5},{5,4},{6,7},{7,6},{8,9},{9,8},{10,11... | collective-permute-start | bytes 3145736 | tf_op jit(solution)/shard_map/ppermute | solution.py:301
  121.3 1.0 copy-start.9
  139.6 43.8 %copy-start.5 = (bf16[2,128,512]{2,1,0:T(8,128)(2,1)}, bf16[2,128,512]{2,1,0:T(8,128)(2,1)S(1)}, u32[]{:S(2)}) copy-start(bf16[2,128,512]{2,1,0:T(8,128)(2,1)S(1)} %get-tuple-element.22) | copy-start | bytes 786436
  183.4 4.8 %copy-start.8 = (bf16[2,128,512]{2,1,0:T(8,128)(2,1)S(1)}, bf16[2,128,512]{2,1,0:T(8,128)(2,1)}, u32[]{:S(2)}) copy-start(bf16[2,128,512]{2,1,0:T(8,128)(2,1)} %copy-done.7) | copy-start | bytes 786436
  183.9 6.1 %copy-start.6 = (bf16[2,128,512]{2,1,0:T(8,128)(2,1)S(1)}, bf16[2,128,512]{2,1,0:T(8,128)(2,1)}, u32[]{:S(2)}) copy-start(bf16[2,128,512]{2,1,0:T(8,128)(2,1)} %copy-done.5) | copy-start | bytes 786436
  184.7 17.9 %all-to-all-start.4 = ((f32[8,3,8,512]{3,2,1,0:T(8,128)}), f32[8,3,8,512]{3,2,1,0:T(8,128)S(1)}, u32[]{:S(2)}, u32[]{:S(2)}) async-start(f32[8,3,8,512]{3,2,1,0:T(8,128)} %copy_bitcast_fusion), calls=%async_computation.4 | async-start | bytes 786432 | tf_op jit(solution)/shard_map/all_to_all | solution.py:323
  188.1 18.7 %copy-start.4 = (bf16[2,128,512]{2,1,0:T(8,128)(2,1)S(1)}, bf16[2,128,512]{2,1,0:T(8,128)(2,1)}, u32[]{:S(2)}) copy-start(bf16[2,128,512]{2,1,0:T(8,128)(2,1)} %copy-done.3) | copy-start | bytes 786436
  189.9 16.9 %collective-permute-start.6 = (bf16[2,128,1024]{2,1,0:T(8,128)(2,1)S(1)}, bf16[2,128,1024]{2,1,0:T(8,128)(2,1)S(1)}, u32[]{:S(2)}, u32[]{:S(2)}) collective-permute-start(bf16[2,128,1024]{2,1,0:T(8,128)(2,1)S(1)} %fusion.2), channel_id=1, source_target_pairs={{0,1},{1,0},{2,3},{3,2},{4,5},{5,4},{6,7},{7,6},{8,9},{9,8},{10,11... | collective-permute-start | bytes 1572872 | tf_op jit(solution)/shard_map/ppermute | solution.py:314
  191.7 16.8 %collective-permute-start.8 = (bf16[2,128,1024]{2,1,0:T(8,128)(2,1)S(1)}, bf16[2,128,1024]{2,1,0:T(8,128)(2,1)S(1)}, u32[]{:S(2)}, u32[]{:S(2)}) collective-permute-start(bf16[2,128,1024]{2,1,0:T(8,128)(2,1)S(1)} %fusion.3), channel_id=1, source_target_pairs={{0,1},{1,0},{2,3},{3,2},{4,5},{5,4},{6,7},{7,6},{8,9},{9,8},{10,11... | collective-permute-start | bytes 1572872 | tf_op jit(solution)/shard_map/ppermute | solution.py:314
  203.4 17.0 %all-to-all-start.5 = ((f32[8,3,8,512]{3,2,1,0:T(8,128)}), f32[8,3,8,512]{3,2,1,0:T(8,128)S(1)}, u32[]{:S(2)}, u32[]{:S(2)}) async-start(f32[8,3,8,512]{3,2,1,0:T(8,128)} %total.1), calls=%async_computation.5 | async-start | bytes 786432 | tf_op jit(solution)/shard_map/all_to_all | solution.py:324
Sparse Core Ops, SparseCore 0:
  10.4 67.0 all-gather.1

commit v5 on v4

--- a/solution.py
+++ b/solution.py
@@ -92,11 +92,16 @@
 def attention_kernel(has_before, core_ref, *refs):
     xo, xt, uo, ut, no, nt, wq, wk, wv = refs[:9]
     before = refs[9] if has_before else None
-    gqo, gqt, sums, q_s, k_s, v_s, gq_s, gkv_s = refs[9 + has_before :]
+    gqo, gqt, sums, q_s, k_s, v_s, gq_s, gkv_s, *early = refs[9 + has_before :]
     prompts, half, channels = xo.shape
     layers, _, rows, _ = no.shape
     part = layers * rows
     width = wq.shape[1]
+    if has_before:
+        before_s, arrived = early
+        at_step = pl.multiple_of(pl.program_id(0) * width, width)
+        fetch = pltpu.make_async_copy(before.at[:, :, pl.ds(at_step, width)], before_s, arrived)
+        fetch.start()
     tokens, maps = (xo, xt), (no, nt)
     for i in range(2):
         x = tokens[i][...].reshape(prompts * half, channels)
@@ -160,6 +165,8 @@
         later = start(*units[i + 1]) if i + 1 < len(units) else None
         finish(*unit, *held)
         held = later
+    if has_before:
+        fetch.wait()
     gq_all = gq_s[...].reshape(2 * prompts * half, width)
     gkv_all = gkv_s[...].reshape(2 * prompts * part, 2 * width)
     block = 256
@@ -173,7 +180,7 @@
             if before is None:
                 sums[i, at] = total
             else:
-                total = (total + before[i, at]).astype(BF16)
+                total = (total + before_s[i, at]).astype(BF16)
                 share = sums.shape[2]
                 own = begin // share
                 sums[own : own + block // share, i] = total.reshape(
@@ -212,7 +219,7 @@
             grid=(steps,),
             in_specs=[token_spec, token_spec, up_spec, up_spec, map_spec, map_spec]
             + w_specs
-            + [wide_spec] * has_before,
+            + [whole(pl.ANY)] * has_before,
             out_specs=[grad_spec, grad_spec, sum_spec],
             scratch_shapes=[
                 pltpu.VMEM((2, prompts, half, step), BF16),
@@ -220,7 +227,8 @@
                 pltpu.VMEM((2, layers, prompts, rows, step), BF16),
                 pltpu.VMEM((2, prompts, half, step), BF16),
                 pltpu.VMEM((2, layers, prompts, rows, 2 * step), BF16),
-            ],
+            ]
+            + [pltpu.VMEM((3, channels, step), F32), pltpu.SemaphoreType.DMA] * has_before,
         ),
         compiler_params=pltpu.CompilerParams(vmem_limit_bytes=50 * 2**20),
         cost_estimate=pl.CostEstimate(

time: 229 us -> 229 us (level)
  no operation moved by 1% of the time
where the time goes in v5:
time: 229 us
  blocking collectives  81.6 us (36%)
  waiting for transfers between devices  54.8 us (24%)
  Pallas kernels  38.4 us (17%)
  starting transfers between devices  26.6 us (12%)
  between operations  14.3 us (6%)
  matrix products  6.81 us (3%)
  local copies, waits for them, and re-layouts  4.39 us (2%)
    all_to_all x1, blocking collectives, per_device(): lax.all_to_all(sums, 'store', split_axis=0, concat_axis=0, tiled=True)  43.9 us
    all_to_all x1, blocking collectives, per_device(): lax.all_to_all(picked[chunk], 'batch', split_axis=0, concat_axis=0, tiled...  37.8 us
    pallas_call x2, Pallas kernels, attention(): pl.pallas_call(functools.partial(attention_kernel, has_before), out_shape...  34 us
    ppermute x3, waiting for transfers between devices, per_device(): lax.ppermute(listed, 'batch', [(z, (z + reach) % layers) for z in range(l...  14 us
    all_to_all x1, waiting for transfers between devices, per_device(): lax.all_to_all(pieces, 'batch', split_axis=0, concat_axis=0, tiled=True)  10.5 us
    all_to_all x1, waiting for transfers between devices, per_device(): lax.all_to_all(total_for_all(crossed), 'batch', split_axis=0, concat_axis...  9.8 us
    all_to_all x1, waiting for transfers between devices, per_device(): lax.all_to_all(spread, 'store', split_axis=0, concat_axis=0, tiled=True)  8.68 us
    all_to_all x1, starting transfers between devices, per_device(): lax.all_to_all(spread, 'store', split_axis=0, concat_axis=0, tiled=True)  7.46 us
  transfers between devices with their start and end apart: 14, of which 9 were waited for; matrix products, arithmetic and copies ran while one was open for 4% of the time, Pallas kernels for 8%

profile of v5, /device:TPU:4, one launch (start us, length us, event | category | flops | bytes accessed | tf_op | source)
XLA Modules:
  0.0 228.5 jit_solution(10464673049680735028)
XLA Ops:
  7.2 0.0 all-gather.2.cloned.1.call-start
  7.2 2.9 %prepare.1 = (bf16[16,4,16,1024]{3,2,1,0:T(8,128)(2,1)}, bf16[64,1536]{1,0:T(8,128)(2,1)}) custom-call(s32[1]{0:T(128)} %bitcast.3.layer_ref, bf16[4,128,1024]{2,1,0:T(8,128)(2,1)} %maps_ref.1, bf16[64,512]{1,0:T(8,128)(2,1)} %wq.1, bf16[64,512]{1,0:T(8,128)(2,1)} %wk.1, bf16[64,512]{1,0:T(8,128)(2,1)} %wv.1), custom_call_target="tpu_custom_call" | custom-call | tf_op jit(solution)/shard_map/prepare/pallas_call | solution.py:37
  10.1 0.0 all-gather.2.cloned.1.call-update
  10.2 7.5 %all-to-all-start = ((bf16[16,4,16,1024]{3,2,1,0:T(8,128)(2,1)}), bf16[16,4,16,1024]{3,2,1,0:T(8,128)(2,1)S(1)}, u32[]{:S(2)}, u32[]{:S(2)}) async-start(bf16[16,4,16,1024]{3,2,1,0:T(8,128)(2,1)} %get-tuple-element.14), calls=%async_computation | async-start | bytes 4194304 | tf_op jit(solution)/shard_map/all_to_all | solution.py:277
  17.6 0.5 collective-permute-start.1
  18.1 0.1 copy.16
  18.2 0.1 reshape.37
  18.3 1.9 collective-permute-start.2
  20.2 5.5 %collective-permute-done.2 = s32[1,8]{1,0:T(1,128)S(1)} collective-permute-done((s32[1,8]{1,0:T(1,128)S(1)}, s32[1,8]{1,0:T(1,128)S(1)}, u32[]{:S(2)}, u32[]{:S(2)}) %collective-permute-start.2) | collective-permute-done | bytes 64 | tf_op jit(solution)/shard_map/ppermute | solution.py:284
  25.7 0.1 collective-permute-start.3
  25.8 5.7 %collective-permute-done.3 = s32[2,8]{1,0:T(2,128)S(1)} collective-permute-done((s32[2,8]{1,0:T(2,128)S(1)}, s32[2,8]{1,0:T(2,128)S(1)}, u32[]{:S(2)}, u32[]{:S(2)}) %collective-permute-start.3) | collective-permute-done | bytes 96 | tf_op jit(solution)/shard_map/ppermute | solution.py:284
  31.5 4.7 %collective-permute-start.4 = (s32[4,8]{1,0:T(4,128)S(1)}, s32[4,8]{1,0:T(4,128)S(1)}, u32[]{:S(2)}, u32[]{:S(2)}) collective-permute-start(s32[4,8]{1,0:T(4,128)S(1)} %pad_add_fusion.1), channel_id=1, source_target_pairs={{0,8},{2,10},{4,12},{6,14},{8,0},{10,2},{12,4},{14,6},{1,9},{3,11}... | collective-permute-start | bytes 392 | tf_op jit(solution)/shard_map/ppermute | solution.py:284
  36.1 2.9 %collective-permute-done.4 = s32[4,8]{1,0:T(4,128)S(1)} collective-permute-done((s32[4,8]{1,0:T(4,128)S(1)}, s32[4,8]{1,0:T(4,128)S(1)}, u32[]{:S(2)}, u32[]{:S(2)}) %collective-permute-start.4) | collective-permute-done | bytes 160 | tf_op jit(solution)/shard_map/ppermute | solution.py:284
  39.1 0.1 copy.17
  39.2 0.1 copy.18
  39.3 0.1 reshape.39.where_ref
  39.4 8.7 %all-to-all-done = bf16[16,4,16,1024]{3,2,1,0:T(8,128)(2,1)S(1)} async-done(((bf16[16,4,16,1024]{3,2,1,0:T(8,128)(2,1)}), bf16[16,4,16,1024]{3,2,1,0:T(8,128)(2,1)S(1)}, u32[]{:S(2)}, u32[]{:S(2)}) %all-to-all-start) | async-done | bytes 2097184 | tf_op jit(solution)/shard_map/all_to_all | solution.py:277
  48.1 0.7 pick.1
  48.8 0.0 copy-start
  48.8 0.0 copy-start.1
  48.8 37.8 %all_to_all.30 = bf16[8,4,16,1024]{3,2,1,0:T(8,128)(2,1)} all-to-all(bf16[8,4,16,1024]{3,2,1,0:T(8,128)(2,1)S(1)} %get-tuple-element.15), channel_id=1, replica_groups=mesh['store'=16,'batch'=8,'space'=2] {'batch'}, dimensions={0} | all-to-all | bytes 2097152 | tf_op jit(solution)/shard_map/all_to_all | solution.py:304
  86.6 4.3 %all-to-all-start.2 = ((bf16[8,4,16,1024]{3,2,1,0:T(8,128)(2,1)}), bf16[8,4,16,1024]{3,2,1,0:T(8,128)(2,1)}, u32[]{:S(2)}, u32[]{:S(2)}) async-start(bf16[8,4,16,1024]{3,2,1,0:T(8,128)(2,1)} %copy-done.2), calls=%async_computation.2 | async-start | bytes 2097152 | tf_op jit(solution)/shard_map/all_to_all | solution.py:304
  90.8 0.1 collective-permute-start.5
  90.9 3.0 %collective-permute-done.5.refs_5_ = bf16[8,2,32,1024]{3,2,1,0:T(8,128)(2,1)} collective-permute-done((bf16[8,2,32,1024]{3,2,1,0:T(8,128)(2,1)}, bf16[8,2,32,1024]{3,2,1,0:T(8,128)(2,1)}, u32[]{:S(2)}, u32[]{:S(2)}) %collective-permute-start.5) | collective-permute-done | bytes 1048608 | tf_op jit(solution)/shard_map/ppermute | solution.py:309
  93.9 17.1 %attention.2 = (bf16[2,128,512]{2,1,0:T(8,128)(2,1)S(1)}, bf16[2,128,512]{2,1,0:T(8,128)(2,1)S(1)}, f32[3,1024,512]{2,1,0:T(8,128)}) custom-call(s32[1]{0:T(128)} %bitcast.core_ref, bf16[4,128,1024]{2,1,0:T(8,128)(2,1)S(1)} %copy-done, bf16[4,128,1024]{2,1,0:T(8,128)(2,1)S(1)} %collective-permute-done.refs_0_.refs_1_, bf16[4,128,1024]{2,1,0:T(8,128)(2,1)S(1)} %copy-done.1, ...), custom_call_target="tpu_custom_call" | custom-call | flops 5368709120 | bytes 16777216 | tf_op jit(solution)/shard_map/attention/pallas_call | solution.py:214
  111.1 0.7 copy-done.3
  111.8 0.7 copy-done.7
  112.5 5.9 %all-to-all-done.2 = bf16[8,4,16,1024]{3,2,1,0:T(8,128)(2,1)} async-done(((bf16[8,4,16,1024]{3,2,1,0:T(8,128)(2,1)}), bf16[8,4,16,1024]{3,2,1,0:T(8,128)(2,1)}, u32[]{:S(2)}, u32[]{:S(2)}) %all-to-all-start.2) | async-done | bytes 1048608 | tf_op jit(solution)/shard_map/all_to_all | solution.py:304
  118.4 0.0 collective-permute-start.7
  118.5 2.9 %collective-permute-done.7.refs_5_ = bf16[8,2,32,1024]{3,2,1,0:T(8,128)(2,1)S(1)} collective-permute-done((bf16[8,2,32,1024]{3,2,1,0:T(8,128)(2,1)}, bf16[8,2,32,1024]{3,2,1,0:T(8,128)(2,1)S(1)}, u32[]{:S(2)}, u32[]{:S(2)}) %collective-permute-start.7) | collective-permute-done | bytes 1048608 | tf_op jit(solution)/shard_map/ppermute | solution.py:309
  121.3 1.0 copy-done.9
  122.3 16.9 %attention.3 = (bf16[2,128,512]{2,1,0:T(8,128)(2,1)S(1)}, bf16[2,128,512]{2,1,0:T(8,128)(2,1)S(1)}, bf16[16,3,64,512]{3,2,1,0:T(8,128)(2,1)}) custom-call(s32[1]{0:T(128)} %bitcast.core_ref, bf16[4,128,1024]{2,1,0:T(8,128)(2,1)S(1)} %copy-done, bf16[4,128,1024]{2,1,0:T(8,128)(2,1)S(1)} %collective-permute-done.refs_0_.refs_1_, ...), custom_call_target="tpu_custom_call" | custom-call | flops 5368709120 | bytes 16777216 | tf_op jit(solution)/shard_map/attention/pallas_call | solution.py:214
  139.2 43.9 %all_to_all.31 = bf16[16,3,64,512]{3,2,1,0:T(8,128)(2,1)S(1)} all-to-all(bf16[16,3,64,512]{3,2,1,0:T(8,128)(2,1)} %get-tuple-element.23), channel_id=1, replica_groups=mesh['store'=16,'batch'=8,'space'=2] {'store'}, dimensions={0} | all-to-all | bytes 6291456 | tf_op jit(solution)/shard_map/all_to_all | solution.py:327
  183.0 0.5 convert_reduce_fusion
  183.5 0.8 copy_bitcast_fusion
  184.3 3.5 %all-to-all-start.4 = ((f32[8,3,8,512]{3,2,1,0:T(8,128)}), f32[8,3,8,512]{3,2,1,0:T(8,128)S(1)}, u32[]{:S(2)}, u32[]{:S(2)}) async-start(f32[8,3,8,512]{3,2,1,0:T(8,128)} %copy_bitcast_fusion), calls=%async_computation.4 | async-start | bytes 786432 | tf_op jit(solution)/shard_map/all_to_all | solution.py:331
  187.8 1.7 fusion.2
  189.5 0.1 collective-permute-start.6
  189.6 1.7 fusion.3
  191.3 0.6 collective-permute-start.8
  191.9 10.5 %all-to-all-done.4.parts_ref = f32[8,3,8,512]{3,2,1,0:T(8,128)S(1)} async-done(((f32[8,3,8,512]{3,2,1,0:T(8,128)}), f32[8,3,8,512]{3,2,1,0:T(8,128)S(1)}, u32[]{:S(2)}, u32[]{:S(2)}) %all-to-all-start.4) | async-done | bytes 393248 | tf_op jit(solution)/shard_map/all_to_all | solution.py:331
  202.4 0.8 total.1
  203.2 3.5 %all-to-all-start.5 = ((f32[8,3,8,512]{3,2,1,0:T(8,128)}), f32[8,3,8,512]{3,2,1,0:T(8,128)S(1)}, u32[]{:S(2)}, u32[]{:S(2)}) async-start(f32[8,3,8,512]{3,2,1,0:T(8,128)} %total.1), calls=%async_computation.5 | async-start | bytes 786432 | tf_op jit(solution)/shard_map/all_to_all | solution.py:332
  206.7 1.7 fusion.5
  208.4 1.7 fusion.4
  210.1 1.1 pad_maximum_fusion
  211.1 9.8 %all-to-all-done.5 = f32[8,3,8,512]{3,2,1,0:T(8,128)S(1)} async-done(((f32[8,3,8,512]{3,2,1,0:T(8,128)}), f32[8,3,8,512]{3,2,1,0:T(8,128)S(1)}, u32[]{:S(2)}, u32[]{:S(2)}) %all-to-all-start.5) | async-done | bytes 393248 | tf_op jit(solution)/shard_map/all_to_all | solution.py:332
  220.9 0.8 slice_bitcast_fusion.5
  (32 shorter events, 0.1 us)
Async XLA Ops:
  7.2 11.0 %copy-start.10 = (s32[4,2]{0,1:T(2,128)S(1)}, s32[4,2]{0,1:T(2,128)}, u32[]{:S(2)}) copy-start(s32[4,2]{0,1:T(2,128)} %param.11) | copy-start | bytes 100
  7.2 11.0 %copy-start.11 = (s32[4,2]{0,1:T(2,128)S(1)}, s32[4,2]{0,1:T(2,128)}, u32[]{:S(2)}) copy-start(s32[4,2]{0,1:T(2,128)} %param.10) | copy-start | bytes 100
  7.2 86.7 %all-gather.2.cloned.1.call-start = ((), (), s32[]{:S(2)}) async-start(), calls=%async_computation.6 | async-start | bytes 3342336 | tf_op jit(solution)/shard_map/all_gather | solution.py:298
  10.2 37.9 %all-to-all-start = ((bf16[16,4,16,1024]{3,2,1,0:T(8,128)(2,1)}), bf16[16,4,16,1024]{3,2,1,0:T(8,128)(2,1)S(1)}, u32[]{:S(2)}, u32[]{:S(2)}) async-start(bf16[16,4,16,1024]{3,2,1,0:T(8,128)(2,1)} %get-tuple-element.14), calls=%async_computation | async-start | bytes 4194304 | tf_op jit(solution)/shard_map/all_to_all | solution.py:277
  17.6 21.7 %collective-permute-start = (bf16[4,128,1024]{2,1,0:T(8,128)(2,1)}, bf16[4,128,1024]{2,1,0:T(8,128)(2,1)S(1)}, u32[]{:S(2)}, u32[]{:S(2)}) collective-permute-start(bf16[4,128,1024]{2,1,0:T(8,128)(2,1)} %refs_0_.3), channel_id=1, source_target_pairs={{0,1},{1,0},{2,3},{3,2},{4,5},{5,4},{6,7},{7,6},{8,9},{9,8},{10,11... | collective-permute-start | bytes 3145736 | tf_op jit(solution)/shard_map/ppermute | solution.py:294
  17.6 21.7 %collective-permute-start.1 = (bf16[4,128,1024]{2,1,0:T(8,128)(2,1)}, bf16[4,128,1024]{2,1,0:T(8,128)(2,1)}, u32[]{:S(2)}, u32[]{:S(2)}) collective-permute-start(bf16[4,128,1024]{2,1,0:T(8,128)(2,1)} %refs_2_.3), channel_id=1, source_target_pairs={{0,1},{1,0},{2,3},{3,2},{4,5},{5,4},{6,7},{7,6},{8,9},{9,8},{10,11... | collective-permute-start | bytes 3145736 | tf_op jit(solution)/shard_map/ppermute | solution.py:295
  18.3 7.4 %collective-permute-start.2 = (s32[1,8]{1,0:T(1,128)S(1)}, s32[1,8]{1,0:T(1,128)S(1)}, u32[]{:S(2)}, u32[]{:S(2)}) collective-permute-start(s32[1,8]{1,0:T(1,128)S(1)} %reshape.37), channel_id=1, source_target_pairs={{0,2},{2,4},{4,6},{6,8},{8,10},{10,12},{12,14},{14,0},{1,3},{3,5},... | collective-permute-start | bytes 104 | tf_op jit(solution)/shard_map/ppermute | solution.py:284
  25.7 5.8 %collective-permute-start.3 = (s32[2,8]{1,0:T(2,128)S(1)}, s32[2,8]{1,0:T(2,128)S(1)}, u32[]{:S(2)}, u32[]{:S(2)}) collective-permute-start(s32[2,8]{1,0:T(2,128)S(1)} %pad_add_fusion.2), channel_id=1, source_target_pairs={{0,4},{2,6},{4,8},{6,10},{8,12},{10,14},{12,0},{14,2},{1,5},{3,7},... | collective-permute-start | bytes 200 | tf_op jit(solution)/shard_map/ppermute | solution.py:284
  31.5 7.6 %collective-permute-start.4 = (s32[4,8]{1,0:T(4,128)S(1)}, s32[4,8]{1,0:T(4,128)S(1)}, u32[]{:S(2)}, u32[]{:S(2)}) collective-permute-start(s32[4,8]{1,0:T(4,128)S(1)} %pad_add_fusion.1), channel_id=1, source_target_pairs={{0,8},{2,10},{4,12},{6,14},{8,0},{10,2},{12,4},{14,6},{1,9},{3,11}... | collective-permute-start | bytes 392 | tf_op jit(solution)/shard_map/ppermute | solution.py:284
  48.7 37.8 %copy-start.2 = (bf16[8,4,16,1024]{3,2,1,0:T(8,128)(2,1)}, bf16[8,4,16,1024]{3,2,1,0:T(8,128)(2,1)S(1)}, u32[]{:S(2)}) copy-start(bf16[8,4,16,1024]{3,2,1,0:T(8,128)(2,1)S(1)} %get-tuple-element.19) | copy-start | bytes 3145732
  48.8 45.2 %copy-start = (bf16[4,128,1024]{2,1,0:T(8,128)(2,1)S(1)}, bf16[4,128,1024]{2,1,0:T(8,128)(2,1)}, u32[]{:S(2)}) copy-start(bf16[4,128,1024]{2,1,0:T(8,128)(2,1)} %refs_0_.3) | copy-start | bytes 3145732
  48.8 45.2 %copy-start.1 = (bf16[4,128,1024]{2,1,0:T(8,128)(2,1)S(1)}, bf16[4,128,1024]{2,1,0:T(8,128)(2,1)}, u32[]{:S(2)}) copy-start(bf16[4,128,1024]{2,1,0:T(8,128)(2,1)} %refs_2_.3) | copy-start | bytes 3145732
  86.6 31.9 %all-to-all-start.2 = ((bf16[8,4,16,1024]{3,2,1,0:T(8,128)(2,1)}), bf16[8,4,16,1024]{3,2,1,0:T(8,128)(2,1)}, u32[]{:S(2)}, u32[]{:S(2)}) async-start(bf16[8,4,16,1024]{3,2,1,0:T(8,128)(2,1)} %copy-done.2), calls=%async_computation.2 | async-start | bytes 2097152 | tf_op jit(solution)/shard_map/all_to_all | solution.py:304
  90.8 3.1 %collective-permute-start.5 = (bf16[8,2,32,1024]{3,2,1,0:T(8,128)(2,1)}, bf16[8,2,32,1024]{3,2,1,0:T(8,128)(2,1)}, u32[]{:S(2)}, u32[]{:S(2)}) collective-permute-start(bf16[8,2,32,1024]{3,2,1,0:T(8,128)(2,1)} %bitcast.30), channel_id=1, source_target_pairs={{0,1},{1,0},{2,3},{3,2},{4,5},{5,4},{6,7},{7,6},{8,9},{9,8},{10,11... | collective-permute-start | bytes 3145736 | tf_op jit(solution)/shard_map/ppermute | solution.py:309
  111.1 0.7 copy-start.3
  111.8 0.7 copy-start.7
  118.4 2.9 %collective-permute-start.7 = (bf16[8,2,32,1024]{3,2,1,0:T(8,128)(2,1)}, bf16[8,2,32,1024]{3,2,1,0:T(8,128)(2,1)S(1)}, u32[]{:S(2)}, u32[]{:S(2)}) collective-permute-start(bf16[8,2,32,1024]{3,2,1,0:T(8,128)(2,1)} %hold.1.refs_4_), channel_id=1, source_target_pairs={{0,1},{1,0},{2,3},{3,2},{4,5},{5,4},{6,7},{7,6},{8,9},{9,8},{10,11... | collective-permute-start | bytes 3145736 | tf_op jit(solution)/shard_map/ppermute | solution.py:309
  121.3 1.0 copy-start.9
  139.1 43.9 %copy-start.5 = (bf16[2,128,512]{2,1,0:T(8,128)(2,1)}, bf16[2,128,512]{2,1,0:T(8,128)(2,1)S(1)}, u32[]{:S(2)}) copy-start(bf16[2,128,512]{2,1,0:T(8,128)(2,1)S(1)} %get-tuple-element.22) | copy-start | bytes 786436
  183.0 4.8 %copy-start.8 = (bf16[2,128,512]{2,1,0:T(8,128)(2,1)S(1)}, bf16[2,128,512]{2,1,0:T(8,128)(2,1)}, u32[]{:S(2)}) copy-start(bf16[2,128,512]{2,1,0:T(8,128)(2,1)} %copy-done.7) | copy-start | bytes 786436
  183.5 6.1 %copy-start.6 = (bf16[2,128,512]{2,1,0:T(8,128)(2,1)S(1)}, bf16[2,128,512]{2,1,0:T(8,128)(2,1)}, u32[]{:S(2)}) copy-start(bf16[2,128,512]{2,1,0:T(8,128)(2,1)} %copy-done.5) | copy-start | bytes 786436
  184.3 18.1 %all-to-all-start.4 = ((f32[8,3,8,512]{3,2,1,0:T(8,128)}), f32[8,3,8,512]{3,2,1,0:T(8,128)S(1)}, u32[]{:S(2)}, u32[]{:S(2)}) async-start(f32[8,3,8,512]{3,2,1,0:T(8,128)} %copy_bitcast_fusion), calls=%async_computation.4 | async-start | bytes 786432 | tf_op jit(solution)/shard_map/all_to_all | solution.py:331
  187.8 18.9 %copy-start.4 = (bf16[2,128,512]{2,1,0:T(8,128)(2,1)S(1)}, bf16[2,128,512]{2,1,0:T(8,128)(2,1)}, u32[]{:S(2)}) copy-start(bf16[2,128,512]{2,1,0:T(8,128)(2,1)} %copy-done.3) | copy-start | bytes 786436
  189.5 17.1 %collective-permute-start.6 = (bf16[2,128,1024]{2,1,0:T(8,128)(2,1)S(1)}, bf16[2,128,1024]{2,1,0:T(8,128)(2,1)S(1)}, u32[]{:S(2)}, u32[]{:S(2)}) collective-permute-start(bf16[2,128,1024]{2,1,0:T(8,128)(2,1)S(1)} %fusion.2), channel_id=1, source_target_pairs={{0,1},{1,0},{2,3},{3,2},{4,5},{5,4},{6,7},{7,6},{8,9},{9,8},{10,11... | collective-permute-start | bytes 1572872 | tf_op jit(solution)/shard_map/ppermute | solution.py:322
  191.3 17.0 %collective-permute-start.8 = (bf16[2,128,1024]{2,1,0:T(8,128)(2,1)S(1)}, bf16[2,128,1024]{2,1,0:T(8,128)(2,1)S(1)}, u32[]{:S(2)}, u32[]{:S(2)}) collective-permute-start(bf16[2,128,1024]{2,1,0:T(8,128)(2,1)S(1)} %fusion.3), channel_id=1, source_target_pairs={{0,1},{1,0},{2,3},{3,2},{4,5},{5,4},{6,7},{7,6},{8,9},{9,8},{10,11... | collective-permute-start | bytes 1572872 | tf_op jit(solution)/shard_map/ppermute | solution.py:322
  203.2 17.8 %all-to-all-start.5 = ((f32[8,3,8,512]{3,2,1,0:T(8,128)}), f32[8,3,8,512]{3,2,1,0:T(8,128)S(1)}, u32[]{:S(2)}, u32[]{:S(2)}) async-start(f32[8,3,8,512]{3,2,1,0:T(8,128)} %total.1), calls=%async_computation.5 | async-start | bytes 786432 | tf_op jit(solution)/shard_map/all_to_all | solution.py:332
Sparse Core Ops, SparseCore 0:
  10.4 67.0 all-gather.1
